TPU v7x, 128 devices: a whole 4x4x4 slice. The times are simulated.
128 devices in a mesh: ord: 16 (over z, y), lev: 8 (over x, core).
Axes of the slice: x: 4, y: 4, z: 4, core: 2. Of those that a mesh axis runs over, the one named last changes fastest.
Arguments:
- grid_grad: bfloat16 [1280, 136, 2560], P('ord', 'lev'), may hold values from -0.119628906 to 0.119628906
- legendre: bfloat16 [512, 1280, 1280], P(('ord', 'lev')), may hold values from -0.15625 to 0.15625
- cov_root: bfloat16 [1280, 136, 136], P('lev'), may hold values from -0.5 to 0.5
- order_ids: int32 [512], replicated, may hold values from 0 to 1279, as said below
- cycle_map: int32 [1280], replicated, may hold values from 0 to 1279, each once
Outputs:
- control_grad: float32 [1280, 512, 2, 136], P('lev', 'ord')
Inputs may be any that keep to these rules, and one draw needn't show every extreme that they name: `order_ids`: distinct orders; 0 and 1279 are always among them. `cycle_map`: a permutation of the cycles.
All inputs are finite; a program needn't handle non-finite values.
Results may differ from a plain program's by a relative error of at most 0.0047.
Values may be sent and summed in bfloat16 or wider, within the bound.
No kernel may reach another device: no remote copies, remote signals or barrier semaphores. Data moves between devices by JAX's collectives and lax.ppermute only.
A program may use at most 128 MiB of HBM per device.

v0:
```python
import math

import jax
import jax.numpy as jnp
from jax import lax
from jax.sharding import PartitionSpec as P


def fourier_weights(order_ids, lon_count):
    longitudes = jnp.arange(lon_count, dtype=jnp.int32)
    phases = longitudes[:, None] * order_ids[None, :] % lon_count
    angles = phases.astype(jnp.float32) * (2.0 * math.pi / lon_count)
    scales = jnp.where(order_ids == 0, 1.0, 2.0).astype(jnp.float32)
    cosine = scales[None, :] * jnp.cos(angles)
    sine = -scales[None, :] * jnp.sin(angles)
    return jnp.stack([cosine, sine], axis=1).astype(jnp.bfloat16)


def shards(grid_grad, legendre, cov_root, order_ids, cycle_map):
    cycles_dev, lev_dev, lon_count = grid_grad.shape
    orders = order_ids.shape[0]
    ord_count = lax.axis_size("ord")
    lev_count = lax.axis_size("lev")
    orders_dev = orders // (ord_count * lev_count)
    fourier_table = fourier_weights(order_ids, lon_count)
    spectra = jnp.einsum(
        "xcm,rlx->cmrl", fourier_table, grid_grad, preferred_element_type=jnp.float32
    ).astype(jnp.bfloat16)
    blocks = spectra.reshape(2, ord_count * lev_count, orders_dev, cycles_dev * lev_dev)
    shipped = lax.all_to_all(blocks, ("ord", "lev"), split_axis=1, concat_axis=1, tiled=True)
    arrived_grid = shipped.reshape(2, ord_count, lev_count, orders_dev, cycles_dev, lev_dev)
    levels = lev_dev * lev_count
    cycle_total = ord_count * cycles_dev
    stored_rows = arrived_grid.transpose(3, 1, 4, 0, 2, 5).reshape(
        orders_dev, cycle_total, 2 * levels
    )
    row_of_cycle = (
        jnp.zeros((cycle_total,), jnp.int32)
        .at[cycle_map]
        .set(jnp.arange(cycle_total, dtype=jnp.int32))
    )
    cycle_rows = jnp.take(stored_rows, row_of_cycle, axis=1)
    position = lax.axis_index("ord") * lev_count + lax.axis_index("lev")
    own_orders = lax.dynamic_slice_in_dim(order_ids, position * orders_dev, orders_dev, 0)
    degree_count = legendre.shape[1]
    degrees = jnp.arange(degree_count, dtype=jnp.int32)
    keep = degrees[None, :, None] >= own_orders[:, None, None]
    masked_legendre = jnp.where(keep, legendre, jnp.zeros_like(legendre))
    coefficients = jnp.einsum(
        "mnr,mrk->mnk", masked_legendre, cycle_rows, preferred_element_type=jnp.float32
    ).astype(jnp.bfloat16)
    arrived = lax.all_to_all(coefficients, "lev", split_axis=1, concat_axis=0, tiled=True)
    spectral = arrived.reshape(arrived.shape[0], arrived.shape[1], 2, levels)
    return jnp.einsum("mncl,nlk->nmck", spectral, cov_root, preferred_element_type=jnp.float32)


def solution(mesh):
    return jax.shard_map(
        shards,
        mesh=mesh,
        in_specs=(
            P("ord", "lev", None),
            P(("ord", "lev"), None, None),
            P("lev", None, None),
            P(),
            P(),
        ),
        out_specs=P("lev", "ord", None, None),
        check_vma=False,
    )
```

profile of v0, /device:TPU:1, one launch (start us, length us, event | category | flops | bytes accessed | tf_op | source)
XLA Modules:
  0.0 313.9 jit_solution(10953831573236092844)
XLA Ops:
  0.7 23.4 %multiply_convert_fusion.1 = (bf16[2560,1,512]{2,0,1:T(8,128)(2,1)S(1)}, bf16[2560,1,512]{2,0,1:T(8,128)(2,1)S(1)}) fusion(s32[512]{0:T(512)} %param.8, f32[512]{0:T(512)S(1)} %get-tuple-element.7, f32[512]{0:T(512)S(1)} %get-tuple-element.8), kind=kLoop, calls=%fused_computation.15 | loop fusion | flops 17039360 | bytes 5249024 | tf_op jit(solution)/shard_map/convert
  24.1 9.6 %fusion.19 = bf16[2,512,80,17]{1,2,3,0:T(8,128)(2,1)S(1)} fusion(bf16[80,17,2560]{2,0,1:T(8,128)(2,1)} %param.5, bf16[2560,1,512]{2,0,1:T(8,128)(2,1)S(1)} %get-tuple-element.6, bf16[2560,1,512]{2,0,1:T(8,128)(2,1)S(1)} %get-tuple-element.5), kind=kOutput, calls=%fused_computation.23 | convolution fusion | flops 7142195200 | bytes 14991360 | tf_op jit(solution)/shard_map/xcm,rlx->cmrl/dot_general | solution.py:26
  33.6 14.9 %copy.17 = bf16[2,512,80,17]{3,2,1,0:T(8,128)(2,1)} copy(bf16[2,512,80,17]{1,2,3,0:T(8,128)(2,1)S(1)} %fusion.19) | data formatting | bytes 5570560 | tf_op jit(solution)/shard_map/convert_element_type | solution.py:28
  48.6 25.0 %reshape.162 = bf16[2,128,4,1360]{3,2,1,0:T(4,128)(2,1)S(1)} reshape(bf16[2,512,80,17]{3,2,1,0:T(8,128)(2,1)} %copy.17) | data formatting | bytes 5570560 | tf_op jit(solution)/shard_map/reshape | solution.py:29
  73.6 2.6 copy.18
  76.1 11.5 %all-to-all-start = ((bf16[2,128,4,1360]{3,2,0,1:T(4,128)(2,1)}), bf16[2,128,4,1360]{3,2,0,1:T(4,128)(2,1)S(1)}, u32[]{:S(2)}, u32[]{:S(2)}) async-start(bf16[2,128,4,1360]{3,2,0,1:T(4,128)(2,1)} %copy.18), calls=%async_computation | async-start | bytes 5767168 | tf_op jit(solution)/shard_map/all_to_all | solution.py:30
  88.4 5.4 %scatter_custom_fusion = s32[1280]{0:T(1024)S(1)} fusion(s32[1280]{0:T(1024)S(1)} %compare_select_fusion.1, s32[1280]{0:T(1024)S(1)} %iota.20, s32[]{:T(128)} %constant.23.clone.1), kind=kCustom, calls=%fused_computation.29 | custom fusion | bytes 5124 | tf_op jit(solution)/shard_map/scatter | solution.py:40
  94.0 32.4 %all-to-all-done = bf16[2,128,4,1360]{3,2,0,1:T(4,128)(2,1)S(1)} async-done(((bf16[2,128,4,1360]{3,2,0,1:T(4,128)(2,1)}), bf16[2,128,4,1360]{3,2,0,1:T(4,128)(2,1)S(1)}, u32[]{:S(2)}, u32[]{:S(2)}) %all-to-all-start) | async-done | bytes 2785312 | tf_op jit(solution)/shard_map/all_to_all | solution.py:30
  126.4 1.9 copy.19
  128.3 27.9 %reshape.163 = bf16[2,16,8,4,80,17]{5,4,2,1,3,0:T(8,128)(2,1)} reshape(bf16[2,128,4,1360]{3,1,2,0:T(8,128)(2,1)} %copy.19) | data formatting | bytes 5570560 | tf_op jit(solution)/shard_map/reshape | solution.py:31
  156.2 21.9 %copy.20 = bf16[4,16,80,2,8,17]{2,1,5,4,3,0:T(8,128)(2,1)} copy(bf16[4,16,80,2,8,17]{5,2,4,1,0,3:T(8,128)(2,1)} %bitcast.33) | data formatting | bytes 5570560 | tf_op jit(solution)/shard_map/transpose | solution.py:34
  178.1 6.9 %reshape.164 = bf16[4,1280,272]{1,2,0:T(8,128)(2,1)S(1)} reshape(bf16[4,16,80,2,8,17]{2,1,5,4,3,0:T(8,128)(2,1)} %copy.20) | data formatting | bytes 5570560 | tf_op jit(solution)/shard_map/reshape | solution.py:34
  185.1 5.9 %copy.21 = bf16[4,1280,272]{2,0,1:T(4,128)(2,1)} copy(bf16[4,1280,272]{1,2,0:T(8,128)(2,1)S(1)} %reshape.164) | data formatting | bytes 5570560 | tf_op jit(solution)/shard_map/reshape | solution.py:34
  191.0 11.8 %gather_fusion = bf16[1280,4,272]{2,1,0:T(4,128)(2,1)} fusion(bf16[4,1280,272]{2,0,1:T(4,128)(2,1)} %copy.21, s32[2048]{0:T(1024)S(1)} %pad_clamp_fusion), kind=kCustom, calls=%fused_computation | custom fusion | bytes 5575680 | tf_op jit(solution)/shard_map/jit(_take)/gather | solution.py:42
  202.7 6.5 %select_bitcast_fusion = bf16[4,1280,272]{2,0,1:T(4,128)(2,1)S(1)} fusion(bf16[1280,4,272]{2,1,0:T(4,128)(2,1)} %gather_fusion, pred[1280]{0:T(1024)(128)(4,1)S(1)} %compare_and_fusion), kind=kLoop, calls=%fused_computation.21 | loop fusion | flops 1392640 | bytes 5571840 | tf_op jit(solution)/shard_map/jit(_take)/select_n | solution.py:42
  209.2 7.8 %fusion.14 = bf16[4,1280,272]{1,2,0:T(8,128)(2,1)S(1)} fusion(bf16[4,1280,272]{2,0,1:T(4,128)(2,1)S(1)} %select_bitcast_fusion, bf16[4,1280,1280]{2,1,0:T(8,128)(2,1)} %param.6, pred[4,1280]{1,0:T(4,128)(4,1)S(1)} %iota_compare_fusion), kind=kOutput, calls=%fused_computation.22 | convolution fusion | flops 3573104640 | bytes 18682880 | tf_op jit(solution)/shard_map/mnr,mrk->mnk/dot_general | solution.py:49
  217.0 5.9 %copy.23 = bf16[4,1280,272]{2,0,1:T(4,128)(2,1)} copy(bf16[4,1280,272]{1,2,0:T(8,128)(2,1)S(1)} %fusion.14) | data formatting | bytes 5570560 | tf_op jit(solution)/shard_map/convert_element_type | solution.py:51
  222.9 5.6 %all-to-all-start.1 = ((bf16[4,1280,272]{2,0,1:T(4,128)(2,1)}), bf16[4,1280,272]{2,0,1:T(4,128)(2,1)}, u32[]{:S(2)}, u32[]{:S(2)}) async-start(bf16[4,1280,272]{2,0,1:T(4,128)(2,1)} %copy.23), calls=%async_computation.1 | async-start | bytes 7864320 | tf_op jit(solution)/shard_map/all_to_all | solution.py:52
  228.5 17.7 %copy.30 = bf16[160,136,136,1]{2,1,3,0:T(8,128)(2,1)} copy(bf16[160,136,136,1]{0,2,1,3:T(8,128)(2,1)} %bitcast.35) | data formatting | bytes 11837440 | tf_op args[2]
  246.2 28.4 %all-to-all-done.1 = bf16[4,1280,272]{2,0,1:T(4,128)(2,1)} async-done(((bf16[4,1280,272]{2,0,1:T(4,128)(2,1)}), bf16[4,1280,272]{2,0,1:T(4,128)(2,1)}, u32[]{:S(2)}, u32[]{:S(2)}) %all-to-all-start.1) | async-done | bytes 2785312 | tf_op jit(solution)/shard_map/all_to_all | solution.py:52
  274.6 7.5 %copy.32 = bf16[4,8,160,272]{2,3,0,1:T(8,128)(2,1)} copy(bf16[4,8,160,272]{3,0,2,1:T(4,128)(2,1)} %bitcast.5) | data formatting | bytes 5570560 | tf_op jit(solution)/shard_map/all_to_all | solution.py:52
  282.1 8.7 %copy.26 = bf16[32,160,2,136]{3,0,2,1:T(8,128)(2,1)} copy(bf16[32,160,2,136]{1,3,2,0:T(8,128)(2,1)} %bitcast.34) | data formatting | bytes 5570560 | tf_op jit(solution)/shard_map/reshape | solution.py:53
  290.9 11.4 %fusion.27 = f32[160,32,2,136]{3,1,2,0:T(8,128)} fusion(bf16[32,160,2,136]{3,0,2,1:T(8,128)(2,1)} %copy.26, bf16[160,136,136,1]{2,1,3,0:T(8,128)(2,1)} %copy.30), kind=kOutput, calls=%fused_computation.35 | convolution fusion | flops 378798080 | bytes 14274560 | tf_op jit(solution)/shard_map/mncl,nlk->nmck/dot_general | solution.py:54
  302.2 11.6 %copy.28 = f32[160,32,2,136]{0,3,2,1:T(8,128)} copy(f32[160,32,2,136]{3,1,2,0:T(8,128)} %fusion.27) | data formatting | bytes 11141120 | tf_op jit(solution)/shard_map/mncl,nlk->nmck/dot_general | solution.py:54
  (10 shorter events, 1.6 us)
Async XLA Ops:
  73.6 14.9 %copy-start = (s32[1280]{0:T(1024)S(1)}, s32[1280]{0:T(1024)}, u32[]{:S(2)}) copy-start(s32[1280]{0:T(1024)} %param.9) | copy-start | bytes 15364
  76.1 50.2 %all-to-all-start = ((bf16[2,128,4,1360]{3,2,0,1:T(4,128)(2,1)}), bf16[2,128,4,1360]{3,2,0,1:T(4,128)(2,1)S(1)}, u32[]{:S(2)}, u32[]{:S(2)}) async-start(bf16[2,128,4,1360]{3,2,0,1:T(4,128)(2,1)} %copy.18), calls=%async_computation | async-start | bytes 5767168 | tf_op jit(solution)/shard_map/all_to_all | solution.py:30
  222.9 51.7 %all-to-all-start.1 = ((bf16[4,1280,272]{2,0,1:T(4,128)(2,1)}), bf16[4,1280,272]{2,0,1:T(4,128)(2,1)}, u32[]{:S(2)}, u32[]{:S(2)}) async-start(bf16[4,1280,272]{2,0,1:T(4,128)(2,1)} %copy.23), calls=%async_computation.1 | async-start | bytes 7864320 | tf_op jit(solution)/shard_map/all_to_all | solution.py:52
where the time goes:
time: 316 us; the launch traced here: 314 us
  local copies, waits for them, and re-layouts  177 us (56%)
  waiting for transfers between devices  60.8 us (19%)
  other arithmetic  30.6 us (10%)
  matrix products  28.7 us (9%)
  starting transfers between devices  17 us (5%)
    all_to_all x1, waiting for transfers between devices, shards(): lax.all_to_all(blocks, ('ord', 'lev'), split_axis=1, concat_axis=1, tiled...  32.4 us
    all_to_all x1, waiting for transfers between devices, shards(): lax.all_to_all(coefficients, 'lev', split_axis=1, concat_axis=0, tiled=True)  28.4 us
    reshape x1, local copies, waits for them, and re-layouts, shards(): shipped.reshape(2, ord_count, lev_count, orders_dev, cycles_dev, lev_dev)  27.9 us
    reshape x2, local copies, waits for them, and re-layouts, shards(): spectra.reshape(2, ord_count * lev_count, orders_dev, cycles_dev * lev_dev)  27.6 us
    another operation x1, other arithmetic  23.4 us
    transpose x1, local copies, waits for them, and re-layouts, shards(): arrived_grid.transpose(3, 1, 4, 0, 2, 5)  21.9 us
    unnamed x3, local copies, waits for them, and re-layouts  17.7 us
    convert_element_type x1, local copies, waits for them, and re-layouts, shards(): spectra = jnp.einsum('xcm,rlx->cmrl', fourier_table, grid_grad, preferred...  14.9 us
  transfers between devices with their start and end apart: 2, of which 2 were waited for; matrix products, arithmetic and copies ran while one was open for 8% of the time, Pallas kernels for 0%

commit v1 on v0

v1 whole, which is shorter than its diff:
```python
import functools
import math

import jax
import jax.numpy as jnp
from jax import lax
from jax.experimental import pallas as pl
from jax.experimental.pallas import tpu as pltpu
from jax.sharding import PartitionSpec as P

MIB = 1024 * 1024
NT = (((1,), (1,)), ((), ()))


def unit_circle(phase, lon_count):
    quarter = lon_count // 4
    turns = jnp.floor(phase * (1.0 / quarter) + 0.5)
    angle = (phase - turns * quarter) * (2.0 * math.pi / lon_count)
    square = angle * angle
    sine = angle * (1.0 + square * (-1.0 / 6 + square * (1.0 / 120 + square * (-1.0 / 5040 + square * (1.0 / 362880)))))
    cosine = 1.0 + square * (-0.5 + square * (1.0 / 24 + square * (-1.0 / 720 + square * (1.0 / 40320))))
    quadrant = turns.astype(jnp.int32) & 3
    swap = (quadrant & 1) == 1
    cos_part = jnp.where(swap, sine, cosine)
    sin_part = jnp.where(swap, cosine, sine)
    cos_out = jnp.where((quadrant == 1) | (quadrant == 2), -cos_part, cos_part)
    sin_out = jnp.where(quadrant >= 2, -sin_part, sin_part)
    return cos_out, sin_out


def fourier_kernel(ids_ref, grid_ref, out_ref, table):
    rows, lon_count = table.shape
    order = ids_ref[...]
    row = lax.broadcasted_iota(jnp.int32, (rows, 1), 0)
    lane = lax.broadcasted_iota(jnp.int32, (rows, 128), 1).astype(jnp.float32)
    offset = jnp.where((row & 1) == 1, lon_count // 4, 0).astype(jnp.float32)
    scale = jnp.where(order == 0.0, 1.0, 2.0)
    cos_far, sin_far = unit_circle(order * 128.0 * lane + offset, lon_count)
    cos_near, sin_near = unit_circle(order * lane, lon_count)
    cos_far, sin_far = cos_far * scale, sin_far * scale
    for a in range(lon_count // 128):
        part = cos_far[:, a:a + 1] * cos_near - sin_far[:, a:a + 1] * sin_near
        table[:, a * 128:(a + 1) * 128] = part.astype(jnp.bfloat16)
    spectra = lax.dot_general(table[...], grid_ref[...], NT, preferred_element_type=jnp.float32)
    out_ref[...] = spectra.reshape(out_ref.shape).astype(jnp.bfloat16)


def fourier(grid_rows, order_ids, dests):
    points, lon_count = grid_rows.shape
    rows = 2 * order_ids.shape[0]
    steps = 4
    per_dest = rows // dests
    ids = jnp.repeat(order_ids, 2)[:, None].astype(jnp.float32)
    return pl.pallas_call(
        fourier_kernel,
        grid=(steps,),
        in_specs=[
            pl.BlockSpec((rows // steps, 1), lambda s: (s, 0)),
            pl.BlockSpec((points, lon_count), lambda s: (0, 0)),
        ],
        out_specs=pl.BlockSpec((dests // steps, per_dest, points), lambda s: (s, 0, 0)),
        out_shape=jax.ShapeDtypeStruct((dests, per_dest, points), jnp.bfloat16),
        scratch_shapes=[pltpu.VMEM((rows // steps, lon_count), jnp.bfloat16)],
        compiler_params=pltpu.CompilerParams(vmem_limit_bytes=48 * MIB),
        name="fourier_analysis",
    )(ids, grid_rows)


def legendre_kernel(ids_ref, got_ref, perm_ref, leg_ref, out_ref, rows_x, rows_z, spectra, rest, *, ord_count, lev_count, lev_dev, cycles_dev, deg_block):
    step = pl.program_id(0)
    orders = leg_ref.shape[0]
    pairs = 2 * orders
    levels = lev_count * lev_dev

    @pl.when(step == 0)
    def _():
        def gather(g, carry):
            for t in range(lev_dev):
                halves = []
                for q in (2 * t, 2 * t + 1):
                    b, l = 2 * g + q // lev_dev, q % lev_dev
                    halves.append(jnp.concatenate([
                        got_ref[a * lev_count + b, :, l * cycles_dev:(l + 1) * cycles_dev].astype(jnp.float32)
                        for a in range(ord_count)
                    ], axis=1))
                both = jnp.concatenate(halves, axis=0).astype(jnp.bfloat16)
                start = pl.multiple_of((2 * g * lev_dev + 2 * t) * pairs, 2 * pairs)
                rows_x[pl.ds(start, 2 * pairs), :] = both
            return carry

        lax.fori_loop(0, lev_count // 2, gather, 0)
        chunk = rows_x.shape[0] // 4

        def permute(g, carry):
            start = pl.multiple_of(g * chunk, 16)
            placed = jnp.dot(rows_x[pl.ds(start, chunk), :], perm_ref[...], preferred_element_type=jnp.float32)
            for t in range(rows_z.shape[0]):
                rows_z[t, pl.ds(start, chunk), :] = placed[:, t * 128:(t + 1) * 128]
            return carry

        lax.fori_loop(0, 4, permute, 0)
        for j in range(orders):
            tails = []
            for c in range(2):
                part = jnp.concatenate([
                    rows_z[t, pl.ds(2 * j + c, levels, stride=pairs), :]
                    for t in range(rows_z.shape[0])], axis=1)
                spectra[j, c * 128:(c + 1) * 128, :] = part[:128].astype(jnp.bfloat16)
                tails.append(part[128:])
            spectra[j, 256:, :] = jnp.concatenate(tails, axis=0).astype(jnp.bfloat16)

    span = leg_ref.shape[1]
    for j in range(orders):
        order = ids_ref[j]
        degree = step * span + lax.broadcasted_iota(jnp.int32, (span, 1), 0)
        used = (step + 1) * span > order

        @pl.when(used)
        def _():
            product = lax.dot_general(leg_ref[j], spectra[j], NT, preferred_element_type=jnp.float32)
            product = jnp.where(degree >= order, product, 0.0)
            for d in range(span // deg_block):
                own = product[d * deg_block:(d + 1) * deg_block]
                for c in range(2):
                    at = (2 * j + c) * deg_block
                    out_ref[d, at:at + deg_block, :] = own[:, c * 128:(c + 1) * 128].astype(jnp.bfloat16)
            rest[j, :, 0:16] = product[:, 256:]

        @pl.when(jnp.logical_not(used))
        def _():
            for d in range(span // deg_block):
                at = 2 * j * deg_block
                out_ref[d, at:at + 2 * deg_block, :] = jnp.zeros((2 * deg_block, 128), jnp.bfloat16)
            rest[j, :, 0:16] = jnp.zeros((span, 16), jnp.float32)

    tail = jnp.concatenate([rest[j, :, 0:16] for j in range(orders)], axis=1)
    half = deg_block // 2
    for d in range(span // deg_block):
        first = tail[d * deg_block:d * deg_block + half]
        second = tail[d * deg_block + half:(d + 1) * deg_block]
        out_ref[d, pairs * deg_block:, :] = jnp.concatenate([first, second], axis=1).astype(jnp.bfloat16)


def legendre_sums(own_orders, arrived, perm, legendre, ord_count, lev_count, lev_dev, cycles_dev):
    orders, degrees, cycles = legendre.shape
    deg_block = degrees // lev_count
    per_step = 2
    steps = lev_count // per_step
    packed = (2 * orders) * deg_block + deg_block // 2
    rows = 2 * orders * lev_count * lev_dev
    kernel = functools.partial(
        legendre_kernel, ord_count=ord_count, lev_count=lev_count, lev_dev=lev_dev,
        cycles_dev=cycles_dev, deg_block=deg_block)
    return pl.pallas_call(
        kernel,
        grid_spec=pltpu.PrefetchScalarGridSpec(
            num_scalar_prefetch=1,
            grid=(steps,),
            in_specs=[
                pl.BlockSpec(arrived.shape, lambda s, ids: (0, 0, 0)),
                pl.BlockSpec(perm.shape, lambda s, ids: (0, 0)),
                pl.BlockSpec((orders, per_step * deg_block, cycles), lambda s, ids: (0, s, 0)),
            ],
            out_specs=pl.BlockSpec((per_step, packed, 128), lambda s, ids: (s, 0, 0)),
            scratch_shapes=[
                pltpu.VMEM((rows, cycles), jnp.bfloat16),
                pltpu.VMEM((cycles // 128, rows, 128), jnp.float32),
                pltpu.VMEM((orders, 2 * lev_count * lev_dev, cycles), jnp.bfloat16),
                pltpu.VMEM((orders, per_step * deg_block, 128), jnp.float32),
            ],
        ),
        out_shape=jax.ShapeDtypeStruct((lev_count, packed, 128), jnp.bfloat16),
        compiler_params=pltpu.CompilerParams(vmem_limit_bytes=56 * MIB),
        name="legendre_sums",
    )(own_orders, arrived, perm, legendre)


def covariance_kernel(got_ref, cov_hbm, out_ref, cov, main, rest, out_main, out_rest, sems):
    step = pl.program_id(0)
    sources = got_ref.shape[0]
    pairs = main.shape[0] // (sources * cov.shape[0])
    deg_block, levels, _ = cov.shape
    half = deg_block // 2
    pieces = sems.shape[0]
    piece = deg_block // pieces
    rows = sources * pairs

    def load(p):
        return pltpu.make_async_copy(cov_hbm.at[pl.ds(p * piece, piece)], cov.at[pl.ds(p * piece, piece)], sems.at[p])

    @pl.when(step == 0)
    def _():
        for p in range(pieces):
            load(p).start()

        def unpack(s, carry):
            tail = got_ref[s, pairs * deg_block:, :].astype(jnp.float32)
            for r in range(pairs):
                base = pl.multiple_of((s * pairs + r) * deg_block, 16)
                main[pl.ds(base, deg_block), :] = got_ref[s, r * deg_block:(r + 1) * deg_block, :].astype(jnp.float32)
                for h in range(2):
                    at = h * 64 + r * 8
                    moved = tail if at == 0 else pltpu.roll(tail, 128 - at, 1)
                    rest[pl.ds(base + h * half, half), :] = moved
            return carry

        lax.fori_loop(0, sources, unpack, 0)
        for p in range(pieces):
            load(p).wait()

            def multiply(i, carry):
                n = p * piece + i
                left = jnp.concatenate([
                    main[pl.ds(n, rows, stride=deg_block), :],
                    rest[pl.ds(n, rows, stride=deg_block), :]], axis=1)[:, :levels].astype(jnp.bfloat16)
                product = jnp.dot(left, cov[n], preferred_element_type=jnp.float32)
                out_main[pl.ds(n, rows, stride=deg_block), :] = product[:, :128]
                out_rest[pl.ds(n, rows, stride=deg_block), :] = product[:, 128:]
                return carry

            lax.fori_loop(0, piece, multiply, 0, unroll=4)

    for r in range(pairs):
        base = pl.multiple_of((step * pairs + r) * deg_block, 16)
        out_ref[r // 2, r % 2, 0:128, :] = out_main[pl.ds(base, deg_block), :].T
        out_ref[r // 2, r % 2, 128:, :] = out_rest[pl.ds(base, deg_block), :].T[:levels - 128]


def covariance(arrived, cov, orders):
    sources, packed, _ = arrived.shape
    deg_block, levels, wide = cov.shape
    order_block = orders // sources
    rows = 2 * orders * deg_block
    pieces = 10
    return pl.pallas_call(
        covariance_kernel,
        grid=(sources,),
        in_specs=[
            pl.BlockSpec(arrived.shape, lambda s: (0, 0, 0)),
            pl.BlockSpec(memory_space=pl.ANY),
        ],
        out_specs=pl.BlockSpec((order_block, 2, levels, deg_block), lambda s: (s, 0, 0, 0)),
        out_shape=jax.ShapeDtypeStruct((orders, 2, levels, deg_block), jnp.float32),
        scratch_shapes=[
            pltpu.VMEM((deg_block, levels, wide), jnp.bfloat16),
            pltpu.VMEM((rows, 128), jnp.float32),
            pltpu.VMEM((rows, 128), jnp.float32),
            pltpu.VMEM((rows, 128), jnp.float32),
            pltpu.VMEM((rows, 128), jnp.float32),
            pltpu.SemaphoreType.DMA((pieces,)),
        ],
        compiler_params=pltpu.CompilerParams(vmem_limit_bytes=56 * MIB),
        name="vertical_covariance",
    )(arrived, cov)


def shards(grid_grad, legendre, cov_root, order_ids, cycle_map):
    cycles_dev, lev_dev, lon_count = grid_grad.shape
    orders_dev, degree_count, cycle_total = legendre.shape
    ord_count = lax.axis_size("ord")
    lev_count = lax.axis_size("lev")
    dests = ord_count * lev_count
    grid_rows = grid_grad.transpose(1, 0, 2).reshape(lev_dev * cycles_dev, lon_count)
    spectra = fourier(grid_rows, order_ids, dests)
    arrived = lax.all_to_all(spectra, ("ord", "lev"), split_axis=0, concat_axis=0, tiled=True)
    position = lax.axis_index("ord") * lev_count + lax.axis_index("lev")
    own_orders = lax.dynamic_slice_in_dim(order_ids, position * orders_dev, orders_dev, 0)
    perm = (cycle_map[:, None] == jnp.arange(cycle_total, dtype=jnp.int32)[None, :]).astype(jnp.bfloat16)
    packed = legendre_sums(own_orders, arrived, perm, legendre, ord_count, lev_count, lev_dev, cycles_dev)
    swapped = lax.all_to_all(packed, "lev", split_axis=0, concat_axis=0, tiled=True)
    levels = lev_dev * lev_count
    cov = jnp.pad(cov_root, ((0, 0), (0, 0), (0, 256 - levels)))
    out = covariance(swapped, cov, orders_dev * lev_count)
    return out.transpose(3, 0, 1, 2)


def solution(mesh):
    return jax.shard_map(
        shards,
        mesh=mesh,
        in_specs=(
            P("ord", "lev", None),
            P(("ord", "lev"), None, None),
            P("lev", None, None),
            P(),
            P(),
        ),
        out_specs=P("lev", "ord", None, None),
        check_vma=False,
    )
```

time: 316 us -> 159 us (0.50)
  local copies, waits for them, and re-layouts: 177 us -> 33.2 us
  Pallas kernels: 0 us -> 65.3 us
  matrix products: 28.7 us -> 0 us
  other arithmetic: 30.6 us -> 2.99 us
  waiting for transfers between devices: 60.8 us -> 40.5 us
    reshape x6 -> x0, local copies, waits for them, and re-layouts: 77 us -> none  [the longest x1 27.9 us: shards(): shipped.reshape(2, ord_count, lev_count, orders_dev, cycles_dev, lev_dev)]
    pallas_call x0 -> x3, Pallas kernels: none -> 65.3 us  [the longest x1 24.8 us: covariance(): pl.pallas_call(covariance_kernel, grid=(sources,), in_specs=[pl.BlockSpec...]
    dot_general x3 -> x0, matrix products: 28.7 us -> none  [the longest x1 11.4 us: shards(): jnp.einsum('mncl,nlk->nmck', spectral, cov_root, preferred_element_type=j...]
    another operation x1 -> x0, other arithmetic: 23.4 us -> none
    transpose x1 -> x0, local copies, waits for them, and re-layouts: 21.9 us -> none  [shards(): arrived_grid.transpose(3, 1, 4, 0, 2, 5)]
    convert_element_type x2 -> x1, local copies, waits for them, and re-layouts: 20.8 us -> 0.15 us  [fourier(): ids = jnp.repeat(order_ids, 2)[:, None].astype(jnp.float32)]
    all_to_all x2, waiting for transfers between devices: 60.8 us -> 40.5 us  [the longest x1 35.1 us: shards(): lax.all_to_all(spectra, ('ord', 'lev'), split_axis=0, concat_axis=0, tile...]
    gather x1 -> x0, local copies, waits for them, and re-layouts: 11.8 us -> none  [shards(): cycle_rows = jnp.take(stored_rows, row_of_cycle, axis=1)]
  transfers between devices with their start and end apart: 2 -> 2, of which waited for: 2 -> 2; matrix products, arithmetic and copies ran while one was open for 8% -> 20% of each run, Pallas kernels for 0% -> 0%
where the time goes in v1:
time: 159 us; the launch traced here: 158 us
  Pallas kernels  65.3 us (41%)
  waiting for transfers between devices  40.5 us (25%)
  local copies, waits for them, and re-layouts  33.2 us (21%)
  starting transfers between devices  16.2 us (10%)
  other arithmetic  2.99 us (2%)
    all_to_all x1, waiting for transfers between devices, shards(): lax.all_to_all(spectra, ('ord', 'lev'), split_axis=0, concat_axis=0, tile...  35.1 us
    pallas_call x1, Pallas kernels, covariance(): pl.pallas_call(covariance_kernel, grid=(sources,), in_specs=[pl.BlockSpec...  24.8 us
    unnamed x7, local copies, waits for them, and re-layouts  20.9 us
    pallas_call x1, Pallas kernels, legendre_sums(): pl.pallas_call(kernel, grid_spec=pltpu.PrefetchScalarGridSpec(num_scalar_...  20.6 us
    pallas_call x1, Pallas kernels, fourier(): pl.pallas_call(fourier_kernel, grid=(steps,), in_specs=[pl.BlockSpec((row...  19.9 us
    all_to_all x1, starting transfers between devices, shards(): lax.all_to_all(spectra, ('ord', 'lev'), split_axis=0, concat_axis=0, tile...  11.5 us
    pad x1, local copies, waits for them, and re-layouts, shards(): cov = jnp.pad(cov_root, ((0, 0), (0, 0), (0, 256 - levels)))  10.7 us
    all_to_all x1, waiting for transfers between devices, shards(): lax.all_to_all(packed, 'lev', split_axis=0, concat_axis=0, tiled=True)  5.36 us
  transfers between devices with their start and end apart: 2, of which 2 were waited for; matrix products, arithmetic and copies ran while one was open for 20% of the time, Pallas kernels for 0%

profile of v1, /device:TPU:1, one launch (start us, length us, event | category | flops | bytes accessed | tf_op | source)
XLA Modules:
  0.0 158.3 jit_solution(2377412990024701390)
XLA Ops:
  0.0 0.7 convert_element_type.10
  0.7 0.1 broadcast_in_dim.2
  0.8 0.2 convert_element_type.13.ids_ref
  1.0 0.0 copy-start.2
  1.0 19.9 %fourier_analysis.1 = bf16[128,8,1360]{2,1,0:T(8,128)(2,1)} custom-call(f32[1024,1]{1,0:T(8,128)S(1)} %convert_element_type.13.ids_ref, bf16[1360,2560]{1,0:T(8,128)(2,1)} %bitcast.4), custom_call_target="tpu_custom_call" | custom-call | tf_op jit(solution)/shard_map/fourier_analysis/pallas_call | solution.py:54
  20.9 11.5 %all-to-all-start = ((bf16[128,8,1360]{2,1,0:T(8,128)(2,1)}), bf16[128,8,1360]{2,1,0:T(8,128)(2,1)S(1)}, u32[]{:S(2)}, u32[]{:S(2)}) async-start(bf16[128,8,1360]{2,1,0:T(8,128)(2,1)} %fourier_analysis.1), calls=%async_computation | async-start | bytes 5767168 | tf_op jit(solution)/shard_map/all_to_all | solution.py:265
  32.4 1.3 dynamic_slice.3.ids_ref
  33.7 0.0 copy-done.2
  33.7 2.3 %fusion.perm_ref = bf16[1280,1280]{1,0:T(8,128)(2,1)} fusion(s32[1280]{0:T(1024)S(1)} %copy-done.2), kind=kLoop, calls=%fused_computation.1 | loop fusion | flops 3276800 | bytes 3281920 | tf_op jit(solution)/shard_map/convert_element_type | solution.py:268
  36.0 35.1 %all-to-all-done.got_ref = bf16[128,8,1360]{2,1,0:T(8,128)(2,1)S(1)} async-done(((bf16[128,8,1360]{2,1,0:T(8,128)(2,1)}), bf16[128,8,1360]{2,1,0:T(8,128)(2,1)S(1)}, u32[]{:S(2)}, u32[]{:S(2)}) %all-to-all-start) | async-done | bytes 2785312 | tf_op jit(solution)/shard_map/all_to_all | solution.py:265
  71.1 0.0 copy-start
  71.1 1.6 copy-done
  72.7 20.6 %legendre_sums.1 = bf16[8,1360,128]{2,1,0:T(8,128)(2,1)} custom-call(s32[4]{0:T(128)} %dynamic_slice.3.ids_ref, bf16[128,8,1360]{2,1,0:T(8,128)(2,1)} %copy-done, bf16[1280,1280]{1,0:T(8,128)(2,1)} %fusion.perm_ref, bf16[4,1280,1280]{2,1,0:T(8,128)(2,1)} %leg_ref.1), custom_call_target="tpu_custom_call" | custom-call | tf_op jit(solution)/shard_map/legendre_sums/pallas_call | solution.py:154
  93.3 4.7 %all-to-all-start.1 = ((bf16[8,1360,128]{2,1,0:T(8,128)(2,1)}), bf16[8,1360,128]{2,1,0:T(8,128)(2,1)S(1)}, u32[]{:S(2)}, u32[]{:S(2)}) async-start(bf16[8,1360,128]{2,1,0:T(8,128)(2,1)} %legendre_sums.1), calls=%async_computation.1 | async-start | bytes 5570560 | tf_op jit(solution)/shard_map/all_to_all | solution.py:270
  98.0 17.6 %copy.8 = bf16[160,136,136]{2,1,0:T(8,128)(2,1)} copy(bf16[160,136,136]{0,2,1:T(8,128)(2,1)} %param.7) | data formatting | bytes 11837440 | tf_op args[2]
  115.6 10.7 %pad.4.cov_hbm = bf16[160,136,256]{2,1,0:T(8,128)(2,1)} pad(bf16[160,136,136]{2,1,0:T(8,128)(2,1)} %copy.8, bf16[]{:T(256)} %constant.18.clone.1), padding=0_0x0_0x0_120 | pad | bytes 17059842 | tf_op jit(solution)/shard_map/jit(_pad)/pad | solution.py:272
  126.3 5.4 %all-to-all-done.1.got_ref = bf16[8,1360,128]{2,1,0:T(8,128)(2,1)S(1)} async-done(((bf16[8,1360,128]{2,1,0:T(8,128)(2,1)}), bf16[8,1360,128]{2,1,0:T(8,128)(2,1)S(1)}, u32[]{:S(2)}, u32[]{:S(2)}) %all-to-all-start.1) | async-done | bytes 2785312 | tf_op jit(solution)/shard_map/all_to_all | solution.py:270
  131.7 0.0 copy-start.1
  131.7 1.7 %copy-done.1 = bf16[8,1360,128]{2,1,0:T(8,128)(2,1)} copy-done((bf16[8,1360,128]{2,1,0:T(8,128)(2,1)}, bf16[8,1360,128]{2,1,0:T(8,128)(2,1)S(1)}, u32[]{:S(2)}) %copy-start.1) | copy-done | bytes 2785304
  133.4 24.8 %vertical_covariance.1 = f32[32,2,136,160]{3,2,1,0:T(8,128)} custom-call(bf16[8,1360,128]{2,1,0:T(8,128)(2,1)} %copy-done.1, bf16[160,136,256]{2,1,0:T(8,128)(2,1)} %pad.4.cov_hbm), custom_call_target="tpu_custom_call" | custom-call | tf_op jit(solution)/shard_map/vertical_covariance/pallas_call | solution.py:235
Async XLA Ops:
  1.0 32.7 %copy-start.2 = (s32[1280]{0:T(1024)S(1)}, s32[1280]{0:T(1024)}, u32[]{:S(2)}) copy-start(s32[1280]{0:T(1024)} %param.9) | copy-start | bytes 15364
  20.9 50.3 %all-to-all-start = ((bf16[128,8,1360]{2,1,0:T(8,128)(2,1)}), bf16[128,8,1360]{2,1,0:T(8,128)(2,1)S(1)}, u32[]{:S(2)}, u32[]{:S(2)}) async-start(bf16[128,8,1360]{2,1,0:T(8,128)(2,1)} %fourier_analysis.1), calls=%async_computation | async-start | bytes 5767168 | tf_op jit(solution)/shard_map/all_to_all | solution.py:265
  71.1 1.6 copy-start
  93.3 38.4 %all-to-all-start.1 = ((bf16[8,1360,128]{2,1,0:T(8,128)(2,1)}), bf16[8,1360,128]{2,1,0:T(8,128)(2,1)S(1)}, u32[]{:S(2)}, u32[]{:S(2)}) async-start(bf16[8,1360,128]{2,1,0:T(8,128)(2,1)} %legendre_sums.1), calls=%async_computation.1 | async-start | bytes 5570560 | tf_op jit(solution)/shard_map/all_to_all | solution.py:270
  131.7 1.7 %copy-start.1 = (bf16[8,1360,128]{2,1,0:T(8,128)(2,1)}, bf16[8,1360,128]{2,1,0:T(8,128)(2,1)S(1)}, u32[]{:S(2)}) copy-start(bf16[8,1360,128]{2,1,0:T(8,128)(2,1)S(1)} %all-to-all-done.1.got_ref) | copy-start | bytes 8355844

commit v2 on v1

v2 whole, which is shorter than its diff:
```python
import functools
import math

import jax
import jax.numpy as jnp
from jax import lax
from jax.experimental import pallas as pl
from jax.experimental.pallas import tpu as pltpu
from jax.sharding import PartitionSpec as P

MIB = 1024 * 1024
FULL = 62 * MIB
NT = (((1,), (1,)), ((), ()))


def cosine(phase, lon_count):
    turns = jnp.floor(phase * (1.0 / lon_count) + 0.5)
    folded = jnp.abs(phase - turns * lon_count)
    angle = (lon_count / 4 - folded) * (2.0 * math.pi / lon_count)
    square = angle * angle
    series = -1.0 / 39916800
    for factor in (1.0 / 362880, -1.0 / 5040, 1.0 / 120, -1.0 / 6, 1.0):
        series = series * square + factor
    return series * angle


def fourier_kernel(ids_ref, grid_hbm, out_ref, table, field, sem):
    step = pl.program_id(0)
    rows, lon_count = table.shape
    blocks = lon_count // 128
    middle = blocks // 2
    group = 16

    @pl.when(step == 0)
    def _():
        load = pltpu.make_async_copy(grid_hbm, field, sem)
        load.start()
        row = lax.broadcasted_iota(jnp.int32, (group, 128), 0)
        lane = lax.broadcasted_iota(jnp.int32, (group, 128), 1).astype(jnp.float32)
        offset = jnp.where((row & 1) == 1, lon_count // 4, 0).astype(jnp.float32)

        def fill(g, carry):
            start = pl.multiple_of(g * group, group)
            order = jnp.broadcast_to(ids_ref[pl.ds(start, group), :], (group, 128))
            scale = jnp.where(order == 0.0, 1.0, 2.0)
            double = 2.0 * cosine(order * 128.0, lon_count)
            below = scale * cosine(order * (lane + (middle - 1) * 128.0) + offset, lon_count)
            above = scale * cosine(order * (lane + middle * 128.0) + offset, lon_count)
            for a, first, second in ((middle - 1, above, below), (middle, below, above)):
                ahead = 1 if a == middle else -1
                while 0 <= a < blocks:
                    table[pl.ds(start, group), a * 128:(a + 1) * 128] = second.astype(jnp.bfloat16)
                    first, second = second, double * second - first
                    a += ahead
            return carry

        lax.fori_loop(0, rows // group, fill, 0, unroll=4)
        load.wait()

    share = rows // pl.num_programs(0)
    mine = pl.ds(pl.multiple_of(step * share, 16), share)
    spectra = lax.dot_general(table[mine, :], field[...], NT, preferred_element_type=jnp.float32)
    out_ref[...] = spectra.reshape(out_ref.shape).astype(jnp.bfloat16)


def fourier(grid_rows, order_ids, dests):
    points, lon_count = grid_rows.shape
    rows = 2 * order_ids.shape[0]
    steps = 4
    per_dest = rows // dests
    ids = jnp.repeat(order_ids, 2)[:, None].astype(jnp.float32)
    return pl.pallas_call(
        fourier_kernel,
        grid=(steps,),
        in_specs=[
            pl.BlockSpec((rows, 1), lambda s: (0, 0)),
            pl.BlockSpec(memory_space=pl.ANY),
        ],
        out_specs=pl.BlockSpec((dests // steps, per_dest, points), lambda s: (s, 0, 0)),
        out_shape=jax.ShapeDtypeStruct((dests, per_dest, points), jnp.bfloat16),
        scratch_shapes=[
            pltpu.VMEM((rows, lon_count), jnp.bfloat16),
            pltpu.VMEM((points, lon_count), jnp.bfloat16),
            pltpu.SemaphoreType.DMA,
        ],
        compiler_params=pltpu.CompilerParams(vmem_limit_bytes=FULL),
        name="fourier_analysis",
    )(ids, grid_rows)


def arrange_kernel(ids_ref, map_ref, leg_ref, out_ref, pick):
    j, step = pl.program_id(0), pl.program_id(1)
    span, cycles = leg_ref.shape[1:]

    @pl.when((j == 0) & (step == 0))
    def _():
        for r in range(0, cycles, 128):
            cycle = r + lax.broadcasted_iota(jnp.int32, (128, cycles), 0)
            pick[r:r + 128, :] = jnp.where(cycle == map_ref[...], 1.0, 0.0).astype(jnp.bfloat16)

    @pl.when((step + 1) * span > ids_ref[j])
    def _():
        out_ref[0] = jnp.dot(leg_ref[0], pick[...], preferred_element_type=jnp.float32).astype(jnp.bfloat16)


def arrange_legendre(own_orders, cycle_map, legendre, span):
    orders, degrees, cycles = legendre.shape
    return pl.pallas_call(
        arrange_kernel,
        grid_spec=pltpu.PrefetchScalarGridSpec(
            num_scalar_prefetch=1,
            grid=(orders, degrees // span),
            in_specs=[
                pl.BlockSpec((1, cycles), lambda j, s, ids: (0, 0)),
                pl.BlockSpec((1, span, cycles), lambda j, s, ids: (j, s, 0)),
            ],
            out_specs=pl.BlockSpec((1, span, cycles), lambda j, s, ids: (j, s, 0)),
            scratch_shapes=[pltpu.VMEM((cycles, cycles), jnp.bfloat16)],
        ),
        out_shape=jax.ShapeDtypeStruct(legendre.shape, jnp.bfloat16),
        compiler_params=pltpu.CompilerParams(vmem_limit_bytes=FULL),
        cost_estimate=pl.CostEstimate(
            flops=2 * orders * degrees * cycles * cycles, bytes_accessed=4 * orders * degrees * cycles, transcendentals=0),
        name="arrange_legendre",
    )(own_orders, cycle_map[None, :], legendre)


def legendre_kernel(ids_ref, got_hbm, leg_hbm, out_ref, got, leg, rows_z, spectra, rest, got_sems, leg_sems, *, ord_count, lev_count, lev_dev, cycles_dev, deg_block):
    step = pl.program_id(0)
    orders = leg.shape[0]
    pairs = 2 * orders
    levels = lev_count * lev_dev
    span = leg.shape[1] // pl.num_programs(0)

    def load_got(b):
        return pltpu.make_async_copy(got_hbm.at[:, b], got.at[:, b], got_sems.at[b])

    def load_leg(p):
        part = pl.ds(pl.multiple_of(p * span, 16), span)
        return pltpu.make_async_copy(leg_hbm.at[:, part, :], leg.at[:, part, :], leg_sems.at[p])

    @pl.when(step == 0)
    def _():
        for b in range(lev_count):
            load_got(b).start()
        for p in range(leg_sems.shape[0]):
            load_leg(p).start()

        def gather(b, carry):
            load_got(b).wait()
            for l in range(lev_dev):
                row = jnp.concatenate([
                    got[a, b, :, l * cycles_dev:(l + 1) * cycles_dev].astype(jnp.float32)
                    for a in range(ord_count)
                ], axis=1)
                for t in range(rows_z.shape[0]):
                    rows_z[t, pl.ds(b * lev_dev + l, pairs, stride=levels), :] = row[:, t * 128:(t + 1) * 128]
            return carry

        lax.fori_loop(0, lev_count, gather, 0)
        for j in range(orders):
            for t in range(rows_z.shape[0]):
                lanes = slice(t * 128, (t + 1) * 128)
                tails = []
                for c in range(2):
                    base = (2 * j + c) * levels
                    spectra[j, c * 128:(c + 1) * 128, lanes] = rows_z[t, base:base + 128, :].astype(jnp.bfloat16)
                    tails.append(rows_z[t, base + 128:base + levels, :])
                spectra[j, 256:, lanes] = jnp.concatenate(tails, axis=0).astype(jnp.bfloat16)

    load_leg(step).wait()
    here = pl.ds(pl.multiple_of(step * span, 16), span)
    for j in range(orders):
        order = ids_ref[j]
        degree = step * span + lax.broadcasted_iota(jnp.int32, (span, 1), 0)
        used = (step + 1) * span > order

        @pl.when(used)
        def _():
            product = lax.dot_general(leg[j, here, :], spectra[j], NT, preferred_element_type=jnp.float32)
            product = jnp.where(degree >= order, product, 0.0)
            for d in range(span // deg_block):
                own = product[d * deg_block:(d + 1) * deg_block]
                for c in range(2):
                    at = (2 * j + c) * deg_block
                    out_ref[d, at:at + deg_block, :] = own[:, c * 128:(c + 1) * 128].astype(jnp.bfloat16)
            rest[j, :, 0:16] = product[:, 256:]

        @pl.when(jnp.logical_not(used))
        def _():
            for d in range(span // deg_block):
                at = 2 * j * deg_block
                out_ref[d, at:at + 2 * deg_block, :] = jnp.zeros((2 * deg_block, 128), jnp.bfloat16)
            rest[j, :, 0:16] = jnp.zeros((span, 16), jnp.float32)

    tail = jnp.concatenate([rest[j, :, 0:16] for j in range(orders)], axis=1)
    half = deg_block // 2
    for d in range(span // deg_block):
        first = tail[d * deg_block:d * deg_block + half]
        second = tail[d * deg_block + half:(d + 1) * deg_block]
        out_ref[d, pairs * deg_block:, :] = jnp.concatenate([first, second], axis=1).astype(jnp.bfloat16)


def legendre_sums(own_orders, arrived, legendre, span, ord_count, lev_count, lev_dev, cycles_dev):
    orders, degrees, cycles = legendre.shape
    deg_block = degrees // lev_count
    per_step = span // deg_block
    steps = degrees // span
    packed = (2 * orders) * deg_block + deg_block // 2
    rows = 2 * orders * lev_count * lev_dev
    kernel = functools.partial(
        legendre_kernel, ord_count=ord_count, lev_count=lev_count, lev_dev=lev_dev,
        cycles_dev=cycles_dev, deg_block=deg_block)
    return pl.pallas_call(
        kernel,
        grid_spec=pltpu.PrefetchScalarGridSpec(
            num_scalar_prefetch=1,
            grid=(steps,),
            in_specs=[pl.BlockSpec(memory_space=pl.ANY)] * 2,
            out_specs=pl.BlockSpec((per_step, packed, 128), lambda s, ids: (s, 0, 0)),
            scratch_shapes=[
                pltpu.VMEM((ord_count, lev_count) + arrived.shape[1:], jnp.bfloat16),
                pltpu.VMEM(legendre.shape, jnp.bfloat16),
                pltpu.VMEM((cycles // 128, rows, 128), jnp.float32),
                pltpu.VMEM((orders, 2 * lev_count * lev_dev, cycles), jnp.bfloat16),
                pltpu.VMEM((orders, span, 128), jnp.float32),
                pltpu.SemaphoreType.DMA((lev_count,)),
                pltpu.SemaphoreType.DMA((steps,)),
            ],
        ),
        out_shape=jax.ShapeDtypeStruct((lev_count, packed, 128), jnp.bfloat16),
        compiler_params=pltpu.CompilerParams(vmem_limit_bytes=FULL),
        name="legendre_sums",
    )(own_orders, arrived.reshape((ord_count, lev_count) + arrived.shape[1:]), legendre)


def degrees_first_kernel(cov_ref, out_ref, front, back):
    step = pl.program_id(0)
    group, levels, deg_block = cov_ref.shape
    last = pl.num_programs(0) - 1

    @pl.when(step < last)
    def _():
        for g in range(group):
            block = cov_ref[g].astype(jnp.float32)
            at = pl.ds(step * group + g, deg_block, stride=levels)
            front[at, :] = block[:128].T
            back[at, :] = jnp.concatenate([block[128:], jnp.zeros((120, deg_block), jnp.float32)], axis=0).T

    @pl.when(step == last)
    def _():
        def narrow(n, carry):
            rows = pl.ds(pl.multiple_of(n * levels, 8), levels)
            out_ref[n, :, 0:128] = front[rows, :].astype(jnp.bfloat16)
            out_ref[n, :, 128:] = back[rows, :].astype(jnp.bfloat16)
            return carry

        lax.fori_loop(0, deg_block, narrow, 0, unroll=4)


def degrees_first(cov_levels):
    levels, _, deg_block = cov_levels.shape
    group = 17
    steps = levels // group
    return pl.pallas_call(
        degrees_first_kernel,
        grid=(steps + 1,),
        in_specs=[pl.BlockSpec((group, levels, deg_block), lambda s: (jnp.minimum(s, steps - 1), 0, 0))],
        out_specs=pl.BlockSpec((deg_block, levels, 256), lambda s: (0, 0, 0), pipeline_mode=pl.Buffered(1)),
        out_shape=jax.ShapeDtypeStruct((deg_block, levels, 256), jnp.bfloat16),
        scratch_shapes=[pltpu.VMEM((deg_block * levels, 128), jnp.float32)] * 2,
        compiler_params=pltpu.CompilerParams(vmem_limit_bytes=FULL),
        cost_estimate=pl.CostEstimate(flops=10**9, bytes_accessed=3 * 10**7, transcendentals=0),
        name="degrees_first",
    )(cov_levels)


def covariance_kernel(got_ref, cov_hbm, out_ref, cov, main, rest, out_main, out_rest, sems, *, pairs):
    step = pl.program_id(0)
    sources = got_ref.shape[0]
    deg_block, levels, _ = cov.shape
    half = deg_block // 2
    rows = sources * pairs
    pitch = main.shape[0] // rows
    pieces = sems.shape[0]
    piece = deg_block // pieces

    def load(p):
        part = pl.ds(p * piece, piece)
        return pltpu.make_async_copy(cov_hbm.at[part], cov.at[part], sems.at[p])

    @pl.when(step == 0)
    def _():
        for p in range(pieces):
            load(p).start()

        def unpack(s, carry):
            tail = got_ref[s, pairs * deg_block:, :].astype(jnp.float32)
            for r in range(pairs):
                base = pl.multiple_of((s * pairs + r) * pitch, 8)
                main[pl.ds(base, deg_block), :] = got_ref[s, r * deg_block:(r + 1) * deg_block, :].astype(jnp.float32)
                for h in range(2):
                    at = h * 64 + r * 8
                    moved = tail if at == 0 else pltpu.roll(tail, 128 - at, 1)
                    rest[pl.ds(base + h * half, half), :] = moved
            return carry

        lax.fori_loop(0, sources, unpack, 0)

        def multiply(n, carry):
            left = jnp.concatenate([
                main[pl.ds(n, rows, stride=pitch), :],
                rest[pl.ds(n, rows, stride=pitch), :]], axis=1)[:, :levels].astype(jnp.bfloat16)
            product = jnp.dot(left, cov[n], preferred_element_type=jnp.float32)
            out_main[pl.ds(n, rows, stride=pitch), :] = product[:, :128]
            out_rest[pl.ds(n, rows, stride=pitch), :] = product[:, 128:]
            return carry

        def share(p, carry):
            load(p).wait()
            for i in range(piece):
                multiply(p * piece + i, carry)
            return carry

        lax.fori_loop(0, pieces, share, 0)

    for r in range(pairs):
        base = pl.multiple_of((step * pairs + r) * pitch, 8)
        out_ref[r // 2, r % 2, 0:128, :] = out_main[pl.ds(base, deg_block), :].T
        out_ref[r // 2, r % 2, 128:, :] = out_rest[pl.ds(base, deg_block), :][:, :levels - 128].T


def covariance(arrived, cov, orders):
    sources = arrived.shape[0]
    deg_block, levels, wide = cov.shape
    order_block = orders // sources
    rows = 2 * orders * (deg_block + 8)
    return pl.pallas_call(
        functools.partial(covariance_kernel, pairs=2 * order_block),
        grid=(sources,),
        in_specs=[
            pl.BlockSpec(memory_space=pltpu.VMEM),
            pl.BlockSpec(memory_space=pl.ANY),
        ],
        out_specs=pl.BlockSpec((order_block, 2, levels, deg_block), lambda s: (s, 0, 0, 0)),
        out_shape=jax.ShapeDtypeStruct((orders, 2, levels, deg_block), jnp.float32),
        scratch_shapes=[pltpu.VMEM(cov.shape, jnp.bfloat16)] + [pltpu.VMEM((rows, 128), jnp.float32)] * 4 + [
            pltpu.SemaphoreType.DMA((10,))],
        compiler_params=pltpu.CompilerParams(vmem_limit_bytes=56 * MIB),
        name="vertical_covariance",
    )(arrived, cov)


def shards(grid_grad, legendre, cov_root, order_ids, cycle_map):
    cycles_dev, lev_dev, lon_count = grid_grad.shape
    orders_dev, degree_count, cycle_total = legendre.shape
    ord_count = lax.axis_size("ord")
    lev_count = lax.axis_size("lev")
    dests = ord_count * lev_count
    grid_rows = grid_grad.transpose(1, 0, 2).reshape(lev_dev * cycles_dev, lon_count)
    spectra = fourier(grid_rows, order_ids, dests)
    position = lax.axis_index("ord") * lev_count + lax.axis_index("lev")
    own_orders = lax.dynamic_slice_in_dim(order_ids, position * orders_dev, orders_dev, 0)
    span = 2 * degree_count // lev_count
    spectra, cycle_map = lax.optimization_barrier((spectra, cycle_map))
    arranged = arrange_legendre(own_orders, cycle_map, legendre, span)
    arrived = lax.all_to_all(spectra, ("ord", "lev"), split_axis=0, concat_axis=0, tiled=True)
    packed = legendre_sums(own_orders, arrived, arranged, span, ord_count, lev_count, lev_dev, cycles_dev)
    swapped = lax.all_to_all(packed, "lev", split_axis=0, concat_axis=0, tiled=True)
    cov = degrees_first(cov_root.transpose(1, 2, 0))
    out = covariance(swapped, cov, orders_dev * lev_count)
    return out.transpose(3, 0, 1, 2)


def solution(mesh):
    return jax.shard_map(
        shards,
        mesh=mesh,
        in_specs=(
            P("ord", "lev", None),
            P(("ord", "lev"), None, None),
            P("lev", None, None),
            P(),
            P(),
        ),
        out_specs=P("lev", "ord", None, None),
        check_vma=False,
    )
```

time: 159 us -> 135 us (0.85)
  local copies, waits for them, and re-layouts: 33.2 us -> 3.02 us
  Pallas kernels: 65.3 us -> 79.9 us
  waiting for transfers between devices: 40.5 us -> 32.6 us
  other arithmetic: 2.99 us -> 0.7 us
    pallas_call x1 -> x3, Pallas kernels: 24.8 us -> 51.5 us  [the longest x1 23.6 us: arrange_legendre(): pl.pallas_call(arrange_kernel, grid_spec=pltpu.PrefetchScalarGridSpec(num...]
    all_to_all x1, waiting for transfers between devices: 35.1 us -> 12.8 us  [shards(): lax.all_to_all(spectra, ('ord', 'lev'), split_axis=0, concat_axis=0, tile...]
    unnamed x7 -> x2, local copies, waits for them, and re-layouts: 20.9 us -> 0.01 us
    all_to_all x1, waiting for transfers between devices: 5.36 us -> 19.7 us  [shards(): lax.all_to_all(packed, 'lev', split_axis=0, concat_axis=0, tiled=True)]
    pad x1 -> x0, local copies, waits for them, and re-layouts: 10.7 us -> none  [shards(): cov = jnp.pad(cov_root, ((0, 0), (0, 0), (0, 256 - levels)))]
    pallas_call x1, Pallas kernels: 20.6 us -> 14.1 us  [legendre_sums(): pl.pallas_call(kernel, grid_spec=pltpu.PrefetchScalarGridSpec(num_scalar_...]
    pallas_call x1, Pallas kernels: 19.9 us -> 14.3 us  [fourier(): pl.pallas_call(fourier_kernel, grid=(steps,), in_specs=[pl.BlockSpec((row...]
    convert_element_type x1 -> x0, other arithmetic: 2.3 us -> none  [shards(): (cycle_map[:, None] == jnp.arange(cycle_total, dtype=jnp.int32)[None, :])...]
  transfers between devices with their start and end apart: 2 -> 2, of which waited for: 2 -> 2; matrix products, arithmetic and copies ran while one was open for 20% -> 1% of each run, Pallas kernels for 0% -> 28%
where the time goes in v2:
time: 135 us; the launch traced here: 134 us
  Pallas kernels  79.9 us (59%)
  waiting for transfers between devices  32.6 us (24%)
  starting transfers between devices  17.3 us (13%)
  local copies, waits for them, and re-layouts  3.02 us (2%)
    pallas_call x1, Pallas kernels, arrange_legendre(): pl.pallas_call(arrange_kernel, grid_spec=pltpu.PrefetchScalarGridSpec(num...  23.6 us
    all_to_all x1, waiting for transfers between devices, shards(): lax.all_to_all(packed, 'lev', split_axis=0, concat_axis=0, tiled=True)  19.7 us
    pallas_call x1, Pallas kernels, fourier(): pl.pallas_call(fourier_kernel, grid=(steps,), in_specs=[pl.BlockSpec((row...  14.3 us
    pallas_call x1, Pallas kernels, degrees_first(): pl.pallas_call(degrees_first_kernel, grid=(steps + 1,), in_specs=[pl.Bloc...  14.1 us
    pallas_call x1, Pallas kernels, legendre_sums(): pl.pallas_call(kernel, grid_spec=pltpu.PrefetchScalarGridSpec(num_scalar_...  14.1 us
    pallas_call x1, Pallas kernels, covariance(): pl.pallas_call(functools.partial(covariance_kernel, pairs=2 * order_block...  13.7 us
    all_to_all x1, waiting for transfers between devices, shards(): lax.all_to_all(spectra, ('ord', 'lev'), split_axis=0, concat_axis=0, tile...  12.8 us
    all_to_all x1, starting transfers between devices, shards(): lax.all_to_all(spectra, ('ord', 'lev'), split_axis=0, concat_axis=0, tile...  11.9 us
  transfers between devices with their start and end apart: 2, of which 2 were waited for; matrix products, arithmetic and copies ran while one was open for 1% of the time, Pallas kernels for 28%

profile of v2, /device:TPU:1, one launch (start us, length us, event | category | flops | bytes accessed | tf_op | source)
XLA Modules:
  0.0 133.5 jit_solution(2842152208029068595)
XLA Ops:
  0.0 0.0 copy-start
  0.0 0.7 convert_element_type.5
  0.7 0.1 broadcast_in_dim.6
  0.8 1.0 convert_element_type.7.ids_ref
  1.8 14.3 %fourier_analysis.1 = bf16[128,8,1360]{2,1,0:T(8,128)(2,1)} custom-call(f32[1024,1]{1,0:T(8,128)} %convert_element_type.7.ids_ref, bf16[1360,2560]{1,0:T(8,128)(2,1)} %bitcast.7), custom_call_target="tpu_custom_call" | custom-call | tf_op jit(solution)/shard_map/fourier_analysis/pallas_call | solution.py:72
  16.1 11.9 %all-to-all-start = ((bf16[128,8,1360]{2,1,0:T(8,128)(2,1)}), bf16[128,8,1360]{2,1,0:T(8,128)(2,1)}, u32[]{:S(2)}, u32[]{:S(2)}) async-start(bf16[128,8,1360]{2,1,0:T(8,128)(2,1)} %fourier_analysis.1), calls=%async_computation | async-start | bytes 5767168 | tf_op jit(solution)/shard_map/all_to_all | solution.py:367
  28.0 1.3 %dynamic_slice.3.ids_ref = s32[4]{0:T(128)} dynamic-slice(s32[512]{0:T(512)} %param.8, s32[]{:T(128)S(6)} %select_n.3), dynamic_slice_sizes={4} | dynamic-slice | bytes 36 | tf_op jit(solution)/shard_map/dynamic_slice | solution.py:363
  29.4 0.0 copy-done
  29.4 0.6 broadcast_in_dim.7.map_ref
  30.0 23.6 %arrange_legendre.1.leg_hbm = bf16[4,1280,1280]{2,1,0:T(8,128)(2,1)} custom-call(s32[4]{0:T(128)} %dynamic_slice.3.ids_ref, s32[1,1280]{1,0:T(1,128)} %broadcast_in_dim.7.map_ref, bf16[4,1280,1280]{2,1,0:T(8,128)(2,1)} %leg_ref.1), custom_call_target="tpu_custom_call" | custom-call | flops 16777216000 | bytes 26214400 | tf_op jit(solution)/shard_map/arrange_legendre/pallas_call | solution.py:108
  53.6 12.8 %all-to-all-done = bf16[128,8,1360]{2,1,0:T(8,128)(2,1)} async-done(((bf16[128,8,1360]{2,1,0:T(8,128)(2,1)}), bf16[128,8,1360]{2,1,0:T(8,128)(2,1)}, u32[]{:S(2)}, u32[]{:S(2)}) %all-to-all-start) | async-done | bytes 2785312 | tf_op jit(solution)/shard_map/all_to_all | solution.py:367
  66.4 14.1 %legendre_sums.1 = bf16[8,1360,128]{2,1,0:T(8,128)(2,1)} custom-call(s32[4]{0:T(128)} %dynamic_slice.3.ids_ref, bf16[16,8,8,1360]{3,2,1,0:T(8,128)(2,1)} %bitcast.2.got_hbm, bf16[4,1280,1280]{2,1,0:T(8,128)(2,1)} %arrange_legendre.1.leg_hbm), custom_call_target="tpu_custom_call" | custom-call | tf_op jit(solution)/shard_map/legendre_sums/pallas_call | solution.py:214
  80.5 5.4 %all-to-all-start.1 = ((bf16[8,1360,128]{2,1,0:T(8,128)(2,1)}), bf16[8,1360,128]{2,1,0:T(8,128)(2,1)}, u32[]{:S(2)}, u32[]{:S(2)}) async-start(bf16[8,1360,128]{2,1,0:T(8,128)(2,1)} %legendre_sums.1), calls=%async_computation.1 | async-start | bytes 5570560 | tf_op jit(solution)/shard_map/all_to_all | solution.py:369
  86.0 14.1 %degrees_first.1.cov_hbm = bf16[160,136,256]{2,1,0:T(8,128)(2,1)} custom-call(bf16[136,136,160]{2,1,0:T(8,128)(2,1)} %bitcast.6), custom_call_target="tpu_custom_call" | custom-call | flops 1000000000 | bytes 30000000 | tf_op jit(solution)/shard_map/degrees_first/pallas_call | solution.py:265
  100.1 19.7 %all-to-all-done.1.got_ref = bf16[8,1360,128]{2,1,0:T(8,128)(2,1)} async-done(((bf16[8,1360,128]{2,1,0:T(8,128)(2,1)}), bf16[8,1360,128]{2,1,0:T(8,128)(2,1)}, u32[]{:S(2)}, u32[]{:S(2)}) %all-to-all-start.1) | async-done | bytes 2785312 | tf_op jit(solution)/shard_map/all_to_all | solution.py:369
  119.8 13.7 %vertical_covariance.1 = f32[32,2,136,160]{3,2,1,0:T(8,128)} custom-call(bf16[8,1360,128]{2,1,0:T(8,128)(2,1)} %all-to-all-done.1.got_ref, bf16[160,136,256]{2,1,0:T(8,128)(2,1)} %degrees_first.1.cov_hbm), custom_call_target="tpu_custom_call" | custom-call | tf_op jit(solution)/shard_map/vertical_covariance/pallas_call | solution.py:338
Async XLA Ops:
  0.0 29.4 %copy-start = (s32[1280]{0:T(1024)S(1)}, s32[1280]{0:T(1024)}, u32[]{:S(2)}) copy-start(s32[1280]{0:T(1024)} %param.9) | copy-start | bytes 15364
  16.1 50.3 %all-to-all-start = ((bf16[128,8,1360]{2,1,0:T(8,128)(2,1)}), bf16[128,8,1360]{2,1,0:T(8,128)(2,1)}, u32[]{:S(2)}, u32[]{:S(2)}) async-start(bf16[128,8,1360]{2,1,0:T(8,128)(2,1)} %fourier_analysis.1), calls=%async_computation | async-start | bytes 5767168 | tf_op jit(solution)/shard_map/all_to_all | solution.py:367
  80.5 39.3 %all-to-all-start.1 = ((bf16[8,1360,128]{2,1,0:T(8,128)(2,1)}), bf16[8,1360,128]{2,1,0:T(8,128)(2,1)}, u32[]{:S(2)}, u32[]{:S(2)}) async-start(bf16[8,1360,128]{2,1,0:T(8,128)(2,1)} %legendre_sums.1), calls=%async_computation.1 | async-start | bytes 5570560 | tf_op jit(solution)/shard_map/all_to_all | solution.py:369

commit v3 on v2

v3 whole, which is shorter than its diff:
```python
import functools
import math

import jax
import jax.numpy as jnp
from jax import lax
from jax.experimental import pallas as pl
from jax.experimental.pallas import tpu as pltpu
from jax.sharding import PartitionSpec as P

MIB = 1024 * 1024
FULL = 62 * MIB
NT = (((1,), (1,)), ((), ()))


def cosine(phase, lon_count):
    turns = jnp.floor(phase * (1.0 / lon_count) + 0.5)
    folded = jnp.abs(phase - turns * lon_count)
    angle = (lon_count / 4 - folded) * (2.0 * math.pi / lon_count)
    square = angle * angle
    series = -1.0 / 39916800
    for factor in (1.0 / 362880, -1.0 / 5040, 1.0 / 120, -1.0 / 6, 1.0):
        series = series * square + factor
    return series * angle


def fourier_kernel(ids_ref, grid_hbm, out_ref, table, field, sem, *, orders_dev, per, half):
    step = pl.program_id(0)
    rows, lon_count = table.shape
    blocks = lon_count // 128
    middle = blocks // 2
    group = 16

    @pl.when(step == 0)
    def _():
        load = pltpu.make_async_copy(grid_hbm, field, sem)
        load.start()
        row = lax.broadcasted_iota(jnp.int32, (group, 128), 0)
        lane = lax.broadcasted_iota(jnp.int32, (group, 128), 1).astype(jnp.float32)
        offset = jnp.where((row & 1) == 1, lon_count // 4, 0).astype(jnp.float32)

        def fill(g, carry):
            start = pl.multiple_of(g * group, group)
            order = jnp.zeros((group, 128), jnp.int32)
            for i in range(group // 2):
                k = g * (group // 2) + i
                order = jnp.where(row // 2 == i, ids_ref[k // per * orders_dev + half * per + k % per], order)
            order = order.astype(jnp.float32)
            scale = jnp.where(order == 0.0, 1.0, 2.0)
            double = 2.0 * cosine(order * 128.0, lon_count)
            below = scale * cosine(order * (lane + (middle - 1) * 128.0) + offset, lon_count)
            above = scale * cosine(order * (lane + middle * 128.0) + offset, lon_count)
            for a, first, second in ((middle - 1, above, below), (middle, below, above)):
                ahead = 1 if a == middle else -1
                while 0 <= a < blocks:
                    table[pl.ds(start, group), a * 128:(a + 1) * 128] = second.astype(jnp.bfloat16)
                    first, second = second, double * second - first
                    a += ahead
            return carry

        lax.fori_loop(0, rows // group, fill, 0, unroll=4)
        load.wait()

    share = rows // pl.num_programs(0)
    mine = pl.ds(pl.multiple_of(step * share, 16), share)
    spectra = lax.dot_general(table[mine, :], field[...], NT, preferred_element_type=jnp.float32)
    out_ref[...] = spectra.reshape(out_ref.shape).astype(jnp.bfloat16)


def fourier(grid_rows, order_ids, dests, per, half):
    points, lon_count = grid_rows.shape
    orders_dev = order_ids.shape[0] // dests
    rows = 2 * dests * per
    steps = per
    kernel = functools.partial(fourier_kernel, orders_dev=orders_dev, per=per, half=half)
    return pl.pallas_call(
        kernel,
        grid_spec=pltpu.PrefetchScalarGridSpec(
            num_scalar_prefetch=1,
            grid=(steps,),
            in_specs=[pl.BlockSpec(memory_space=pl.ANY)],
            out_specs=pl.BlockSpec((dests // steps, 2 * per, points), lambda s, ids: (s, 0, 0)),
            scratch_shapes=[
                pltpu.VMEM((rows, lon_count), jnp.bfloat16),
                pltpu.VMEM((points, lon_count), jnp.bfloat16),
                pltpu.SemaphoreType.DMA,
            ],
        ),
        out_shape=jax.ShapeDtypeStruct((dests, 2 * per, points), jnp.bfloat16),
        compiler_params=pltpu.CompilerParams(vmem_limit_bytes=FULL),
        cost_estimate=pl.CostEstimate(flops=2 * rows * points * lon_count, bytes_accessed=10 * MIB, transcendentals=0),
        name="fourier_analysis",
    )(order_ids, grid_rows)


def arrange_kernel(ids_ref, map_ref, leg_ref, out_ref, pick):
    j, step = pl.program_id(0), pl.program_id(1)
    span, cycles = leg_ref.shape[1:]

    @pl.when((j == 0) & (step == 0))
    def _():
        for r in range(0, cycles, 128):
            cycle = r + lax.broadcasted_iota(jnp.int32, (128, cycles), 0)
            pick[r:r + 128, :] = jnp.where(cycle == map_ref[...], 1.0, 0.0).astype(jnp.bfloat16)

    @pl.when((step + 1) * span > ids_ref[j])
    def _():
        out_ref[0] = jnp.dot(leg_ref[0], pick[...], preferred_element_type=jnp.float32).astype(jnp.bfloat16)


def arrange_legendre(own_orders, cycle_map, legendre, span):
    orders, degrees, cycles = legendre.shape
    return pl.pallas_call(
        arrange_kernel,
        grid_spec=pltpu.PrefetchScalarGridSpec(
            num_scalar_prefetch=1,
            grid=(orders, degrees // span),
            in_specs=[
                pl.BlockSpec((1, cycles), lambda j, s, ids: (0, 0)),
                pl.BlockSpec((1, span, cycles), lambda j, s, ids: (j, jnp.maximum(s, ids[j] // span), 0)),
            ],
            out_specs=pl.BlockSpec((1, span, cycles), lambda j, s, ids: (j, jnp.maximum(s, ids[j] // span), 0)),
            scratch_shapes=[pltpu.VMEM((cycles, cycles), jnp.bfloat16)],
        ),
        out_shape=jax.ShapeDtypeStruct(legendre.shape, jnp.bfloat16),
        compiler_params=pltpu.CompilerParams(vmem_limit_bytes=FULL),
        cost_estimate=pl.CostEstimate(
            flops=2 * orders * degrees * cycles * cycles, bytes_accessed=4 * orders * degrees * cycles, transcendentals=0),
        name="arrange_legendre",
    )(own_orders, cycle_map[None, :], legendre)


def tail_rows(deg_block, per):
    return -(-deg_block * 16 * per // 128 // 16) * 16


def legendre_kernel(ids_ref, dests_ref, got_hbm, leg_hbm, *refs, lev_dev, cycles_dev, deg_block, half):
    count = dests_ref.shape[0]
    outs = refs[:count]
    got, leg, rows_z, spectra, rest, send, got_sems, leg_sems, out_sems = refs[count:]
    ord_count, lev_count = got.shape[:2]
    per = leg.shape[0]
    pairs = 2 * per
    levels = lev_count * lev_dev
    span = 2 * deg_block
    steps = count // 2

    def load_got(b):
        return pltpu.make_async_copy(got_hbm.at[:, b], got.at[:, b], got_sems.at[b])

    def load_leg(k):
        source = leg_hbm.at[pl.ds(half * per, per), pl.ds(pl.multiple_of(dests_ref[k] * deg_block, 16), deg_block), :]
        return pltpu.make_async_copy(source, leg.at[:, pl.ds(k * deg_block, deg_block), :], leg_sems.at[k])

    for b in range(lev_count):
        load_got(b).start()
    def gather(b, carry):
        load_got(b).wait()
        load_leg(b).start()
        for l in range(lev_dev):
            row = jnp.concatenate([
                got[a, b, :, l * cycles_dev:(l + 1) * cycles_dev].astype(jnp.float32) for a in range(ord_count)
            ], axis=1)
            for t in range(rows_z.shape[0]):
                rows_z[t, pl.ds(b * lev_dev + l, pairs, stride=levels), :] = row[:, t * 128:(t + 1) * 128]
        return carry

    lax.fori_loop(0, lev_count, gather, 0)
    for j in range(per):
        for t in range(rows_z.shape[0]):
            lanes = slice(t * 128, (t + 1) * 128)
            tails = []
            for c in range(2):
                base = (2 * j + c) * levels
                spectra[j, c * 128:(c + 1) * 128, lanes] = rows_z[t, base:base + 128, :].astype(jnp.bfloat16)
                tails.append(rows_z[t, base + 128:base + levels, :])
            spectra[j, 256:, lanes] = jnp.concatenate(tails, axis=0).astype(jnp.bfloat16)

    row = lax.broadcasted_iota(jnp.int32, (span, 1), 0)
    groups = 128 // (16 * per)
    chunk = deg_block // groups
    for step in range(steps):
        load_leg(2 * step).wait()
        load_leg(2 * step + 1).wait()
        first, second = dests_ref[2 * step], dests_ref[2 * step + 1]
        degree = jnp.where(row < deg_block, first * deg_block + row, (second - 1) * deg_block + row)
        for j in range(per):
            order = ids_ref[half * per + j]
            used = (first // 2 + 1) * span > order

            @pl.when(used)
            def _():
                here = slice(step * span, (step + 1) * span)
                product = lax.dot_general(leg[j, here, :], spectra[j], NT, preferred_element_type=jnp.float32)
                product = jnp.where(degree >= order, product, 0.0)
                for d in range(2):
                    own = product[d * deg_block:(d + 1) * deg_block]
                    for c in range(2):
                        at = (2 * j + c) * deg_block
                        send[2 * step + d, at:at + deg_block, :] = own[:, c * 128:(c + 1) * 128].astype(jnp.bfloat16)
                rest[j, :, 0:16] = product[:, 256:]

            @pl.when(jnp.logical_not(used))
            def _():
                for d in range(2):
                    at = 2 * j * deg_block
                    send[2 * step + d, at:at + 2 * deg_block, :] = jnp.zeros((2 * deg_block, 128), jnp.bfloat16)
                rest[j, :, 0:16] = jnp.zeros((span, 16), jnp.float32)

        tail = jnp.concatenate([rest[j, :, 0:16] for j in range(per)], axis=1)
        for d in range(2):
            packed = jnp.concatenate([
                tail[d * deg_block + g * chunk:d * deg_block + (g + 1) * chunk] for g in range(groups)], axis=1)
            at = pairs * deg_block
            send[2 * step + d, at:at + chunk, :] = packed.astype(jnp.bfloat16)
            k = 2 * step + d
            pltpu.make_async_copy(send.at[k], outs[k], out_sems.at[k]).start()
    for k in range(count):
        pltpu.make_async_copy(send.at[k], outs[k], out_sems.at[k]).wait()


def legendre_sums(own_orders, dests, arrived, legendre, per, half, lev_dev, cycles_dev):
    _, degrees, cycles = legendre.shape
    ord_count, lev_count = arrived.shape[:2]
    deg_block = degrees // lev_count
    packed = 2 * per * deg_block + tail_rows(deg_block, per)
    kernel = functools.partial(legendre_kernel, lev_dev=lev_dev, cycles_dev=cycles_dev, deg_block=deg_block, half=half)
    anywhere = pl.BlockSpec(memory_space=pl.ANY)
    return pl.pallas_call(
        kernel,
        grid_spec=pltpu.PrefetchScalarGridSpec(
            num_scalar_prefetch=2,
            grid=(),
            in_specs=[anywhere] * 2,
            out_specs=[anywhere] * lev_count,
            scratch_shapes=[
                pltpu.VMEM(arrived.shape, jnp.bfloat16),
                pltpu.VMEM((per, degrees, cycles), jnp.bfloat16),
                pltpu.VMEM((cycles // 128, 2 * per * lev_count * lev_dev, 128), jnp.float32),
                pltpu.VMEM((per, 2 * lev_count * lev_dev, cycles), jnp.bfloat16),
                pltpu.VMEM((per, 2 * deg_block, 128), jnp.float32),
                pltpu.VMEM((lev_count, packed, 128), jnp.bfloat16),
                pltpu.SemaphoreType.DMA((lev_count,)),
                pltpu.SemaphoreType.DMA((lev_count,)),
                pltpu.SemaphoreType.DMA((lev_count,)),
            ],
        ),
        out_shape=[jax.ShapeDtypeStruct((packed, 128), jnp.bfloat16)] * lev_count,
        compiler_params=pltpu.CompilerParams(vmem_limit_bytes=FULL),
        cost_estimate=pl.CostEstimate(flops=3 * 10**9, bytes_accessed=20 * MIB, transcendentals=0),
        name="legendre_sums",
    )(own_orders, dests, arrived, legendre)


def degrees_first_kernel(cov_ref, out_ref, front, back):
    step = pl.program_id(0)
    group, levels, deg_block = cov_ref.shape
    last = pl.num_programs(0) - 1

    @pl.when(step < last)
    def _():
        for g in range(group):
            block = cov_ref[g].astype(jnp.float32)
            at = pl.ds(step * group + g, deg_block, stride=levels)
            front[at, :] = block[:128].T
            back[at, :] = jnp.concatenate([block[128:], jnp.zeros((120, deg_block), jnp.float32)], axis=0).T

    @pl.when(step == last)
    def _():
        def narrow(n, carry):
            rows = pl.ds(pl.multiple_of(n * levels, 8), levels)
            out_ref[n, :, 0:128] = front[rows, :].astype(jnp.bfloat16)
            out_ref[n, :, 128:] = back[rows, :].astype(jnp.bfloat16)
            return carry

        lax.fori_loop(0, deg_block, narrow, 0, unroll=4)


def degrees_first(cov_levels):
    levels, _, deg_block = cov_levels.shape
    group = 17
    steps = levels // group
    return pl.pallas_call(
        degrees_first_kernel,
        grid=(steps + 1,),
        in_specs=[pl.BlockSpec((group, levels, deg_block), lambda s: (jnp.minimum(s, steps - 1), 0, 0))],
        out_specs=pl.BlockSpec((deg_block, levels, 256), lambda s: (0, 0, 0), pipeline_mode=pl.Buffered(1)),
        out_shape=jax.ShapeDtypeStruct((deg_block, levels, 256), jnp.bfloat16),
        scratch_shapes=[pltpu.VMEM((deg_block * levels, 128), jnp.float32)] * 2,
        compiler_params=pltpu.CompilerParams(vmem_limit_bytes=FULL),
        cost_estimate=pl.CostEstimate(flops=10**9, bytes_accessed=3 * 10**7, transcendentals=0),
        name="degrees_first",
    )(cov_levels)


def covariance_kernel(place_ref, *refs, per, count, carried):
    got_hbm, cov_hbm = refs[:count], refs[count]
    out_ref, gots, cov, main, rest, out_main, out_rest, got_sems, cov_sems = refs[count + 1 + carried:]
    step = pl.program_id(0)
    deg_block, levels, _ = cov.shape
    pairs = 2 * per
    groups = 128 // (8 * pairs)
    chunk = deg_block // groups
    rows = count * pairs
    pitch = main.shape[0] // rows
    pieces = cov_sems.shape[0]
    piece = deg_block // pieces

    def load_got(s):
        return pltpu.make_async_copy(got_hbm[s], gots.at[s], got_sems.at[s])

    def load_cov(p):
        part = pl.ds(p * piece, piece)
        return pltpu.make_async_copy(cov_hbm.at[part], cov.at[part], cov_sems.at[p])

    @pl.when(step == 0)
    def _():
        for s in range(count):
            load_got(s).start()
        for p in range(2):
            load_cov(p).start()
        for s in range(count):
            load_got(s).wait()
            at = pairs * deg_block
            tail = gots[s, at:at + chunk, :].astype(jnp.float32)
            for r in range(pairs):
                base = (s * pairs + r) * pitch
                main[base:base + deg_block, :] = gots[s, r * deg_block:(r + 1) * deg_block, :].astype(jnp.float32)
                for g in range(groups):
                    lane = (g * pairs + r) * 8
                    moved = tail if lane == 0 else pltpu.roll(tail, 128 - lane, 1)
                    rest[base + g * chunk:base + (g + 1) * chunk, :] = moved

        def multiply(n, carry):
            left = jnp.concatenate([
                main[pl.ds(n, rows, stride=pitch), :],
                rest[pl.ds(n, rows, stride=pitch), :]], axis=1)[:, :levels].astype(jnp.bfloat16)
            product = jnp.dot(left, cov[n], preferred_element_type=jnp.float32)
            out_main[pl.ds(n, rows, stride=pitch), :] = product[:, :128]
            out_rest[pl.ds(n, rows, stride=pitch), :] = product[:, 128:]
            return carry

        def share(p, carry):
            load_cov(p).wait()

            @pl.when(p + 2 < pieces)
            def _():
                load_cov(p + 2).start()

            for i in range(piece):
                multiply(p * piece + i, carry)
            return carry

        lax.fori_loop(0, pieces, share, 0)

    for r in range(pairs):
        base = pl.multiple_of((step * pairs + r) * pitch, 8)
        out_ref[r // 2, r % 2, 0:128, :] = out_main[pl.ds(base, deg_block), :].T
        out_ref[r // 2, r % 2, 128:, :] = out_rest[pl.ds(base, deg_block), :][:, :levels - 128].T


def covariance(places, arrived, cov, out, orders, per, half, halves):
    count = len(arrived)
    deg_block, levels, wide = cov.shape
    rows = count * 2 * per * (deg_block + 8)
    carried = 0 if out is None else 1
    anywhere = pl.BlockSpec(memory_space=pl.ANY)
    return pl.pallas_call(
        functools.partial(covariance_kernel, per=per, count=count, carried=carried),
        grid_spec=pltpu.PrefetchScalarGridSpec(
            num_scalar_prefetch=1,
            grid=(count,),
            in_specs=[anywhere] * (count + 1 + carried),
            out_specs=pl.BlockSpec((per, 2, levels, deg_block), lambda s, place: (place[s] * halves + half, 0, 0, 0)),
            scratch_shapes=[
                pltpu.VMEM((count,) + arrived[0].shape, jnp.bfloat16),
                pltpu.VMEM(cov.shape, jnp.bfloat16),
            ] + [pltpu.VMEM((rows, 128), jnp.float32)] * 4 + [
                pltpu.SemaphoreType.DMA((count,)),
                pltpu.SemaphoreType.DMA((10,)),
            ],
        ),
        out_shape=jax.ShapeDtypeStruct((orders, 2, levels, deg_block), jnp.float32),
        input_output_aliases={count + 2: 0} if carried else {},
        compiler_params=pltpu.CompilerParams(vmem_limit_bytes=FULL),
        cost_estimate=pl.CostEstimate(flops=2 * 10**9, bytes_accessed=16 * MIB, transcendentals=0),
        name="vertical_covariance",
    )(places, *arrived, cov, *([out] if carried else []))


HALVES = 1


def shards(grid_grad, legendre, cov_root, order_ids, cycle_map):
    cycles_dev, lev_dev, lon_count = grid_grad.shape
    orders_dev, degree_count, cycle_total = legendre.shape
    ord_count = lax.axis_size("ord")
    lev_count = lax.axis_size("lev")
    dests = ord_count * lev_count
    chips = lev_count // 2
    per = orders_dev // HALVES
    lev = lax.axis_index("lev")
    position = lax.axis_index("ord") * lev_count + lev
    own_orders = lax.dynamic_slice_in_dim(order_ids, position * orders_dev, orders_dev, 0)
    grid_rows = grid_grad.transpose(1, 0, 2).reshape(lev_dev * cycles_dev, lon_count)

    near = [(d, f) for d in (1, chips - 1) for f in (0, 1)]
    far = [(d, f) for d in range(2, chips - 1) for f in (0, 1)]
    home = [(0, 1), (0, 0)]
    moves = near + far + home

    def moved(rank, d, f):
        return (rank // 2 + d) % chips * 2 + (rank % 2 + f) % 2

    targets = jnp.stack([moved(lev, d, f) for d, f in moves]).astype(jnp.int32)

    spectra = [fourier(grid_rows, order_ids, dests, per, 0)]
    spectra[0], cycle_map, cov_root = lax.optimization_barrier((spectra[0], cycle_map, cov_root))
    arranged = arrange_legendre(own_orders, cycle_map, legendre, 2 * degree_count // lev_count)
    cov = degrees_first(cov_root.transpose(1, 2, 0))
    arranged, cov = lax.optimization_barrier((arranged, cov))
    arrived = []
    for h in range(HALVES):
        if h > 0:
            spectra.append(fourier(grid_rows, order_ids, dests, per, h))
        blocks = lax.all_to_all(spectra[h], ("ord", "lev"), split_axis=0, concat_axis=0, tiled=True)
        blocks = blocks.reshape((ord_count, lev_count) + blocks.shape[1:])
        packed = legendre_sums(own_orders, targets, blocks, arranged, per, h, lev_dev, cycles_dev)
        sent = dict(zip(moves, packed))
        got = {(0, 0): sent[0, 0]}

        def exchange(some):
            for d, f in some:
                pairs = [(rank, moved(rank, d, f)) for rank in range(lev_count)]
                got[d, f] = lax.ppermute(sent[d, f], "lev", pairs)

        exchange(near + home[:1])
        held = near + far
        tied = lax.optimization_barrier([got[m] for m in near] + [sent[m] for m in far])
        for m, block in zip(held, tied):
            (got if m in near else sent)[m] = block
        exchange(far)
        arrived.append(got)

    out = None
    for h in range(HALVES):
        for some in (home + near, far):
            places = jnp.stack([moved(lev, chips - d, f) for d, f in some]).astype(jnp.int32)
            out = covariance(places, [arrived[h][m] for m in some], cov, out, orders_dev * lev_count, per, h, HALVES)
    return out.transpose(3, 0, 1, 2)


def solution(mesh):
    return jax.shard_map(
        shards,
        mesh=mesh,
        in_specs=(
            P("ord", "lev", None),
            P(("ord", "lev"), None, None),
            P("lev", None, None),
            P(),
            P(),
        ),
        out_specs=P("lev", "ord", None, None),
        check_vma=False,
    )
```

time: 135 us -> 129 us (0.956)
  waiting for transfers between devices: 32.6 us -> 16.5 us
  Pallas kernels: 79.9 us -> 85.4 us
  starting transfers between devices: 17.3 us -> 21.6 us
    all_to_all x2 -> x1, waiting for transfers between devices: 32.6 us -> 2.61 us  [shards(): lax.all_to_all(spectra[h], ('ord', 'lev'), split_axis=0, concat_axis=0, t...]
    ppermute x0 -> x7, waiting for transfers between devices: none -> 13.9 us  [exchange(): got[d, f] = lax.ppermute(sent[d, f], 'lev', pairs)]
    pallas_call x2 -> x3, Pallas kernels: 28 us -> 39.5 us  [the longest x2 24.1 us: covariance(): pl.pallas_call(functools.partial(covariance_kernel, per=per, count=count,...]
    ppermute x0 -> x7, starting transfers between devices: none -> 9.72 us  [exchange(): got[d, f] = lax.ppermute(sent[d, f], 'lev', pairs)]
    all_to_all x2 -> x1, starting transfers between devices: 17.3 us -> 11.9 us  [shards(): lax.all_to_all(spectra[h], ('ord', 'lev'), split_axis=0, concat_axis=0, t...]
    pallas_call x1, Pallas kernels: 23.6 us -> 19.2 us  [arrange_legendre(): pl.pallas_call(arrange_kernel, grid_spec=pltpu.PrefetchScalarGridSpec(num...]
  transfers between devices with their start and end apart: 2 -> 8, of which waited for: 2 -> 4; matrix products, arithmetic and copies ran while one was open for 1% -> 3% of each run, Pallas kernels for 28% -> 37%
where the time goes in v3:
time: 129 us; the launch traced here: 128 us
  Pallas kernels  85.4 us (66%)
  starting transfers between devices  21.6 us (17%)
  waiting for transfers between devices  16.5 us (13%)
  local copies, waits for them, and re-layouts  3.85 us (3%)
    pallas_call x2, Pallas kernels, covariance(): pl.pallas_call(functools.partial(covariance_kernel, per=per, count=count,...  24.1 us
    pallas_call x1, Pallas kernels, arrange_legendre(): pl.pallas_call(arrange_kernel, grid_spec=pltpu.PrefetchScalarGridSpec(num...  19.2 us
    pallas_call x1, Pallas kernels, fourier(): pl.pallas_call(kernel, grid_spec=pltpu.PrefetchScalarGridSpec(num_scalar_...  15.4 us
    pallas_call x1, Pallas kernels, degrees_first(): pl.pallas_call(degrees_first_kernel, grid=(steps + 1,), in_specs=[pl.Bloc...  14 us
    ppermute x7, waiting for transfers between devices, exchange(): got[d, f] = lax.ppermute(sent[d, f], 'lev', pairs)  13.9 us
    pallas_call x1, Pallas kernels, legendre_sums(): pl.pallas_call(kernel, grid_spec=pltpu.PrefetchScalarGridSpec(num_scalar_...  12.7 us
    all_to_all x1, starting transfers between devices, shards(): lax.all_to_all(spectra[h], ('ord', 'lev'), split_axis=0, concat_axis=0, t...  11.9 us
    ppermute x7, starting transfers between devices, exchange(): got[d, f] = lax.ppermute(sent[d, f], 'lev', pairs)  9.72 us
  transfers between devices with their start and end apart: 8, of which 4 were waited for; matrix products, arithmetic and copies ran while one was open for 3% of the time, Pallas kernels for 37%

profile of v3, /device:TPU:1, one launch (start us, length us, event | category | flops | bytes accessed | tf_op | source)
XLA Modules:
  0.0 128.3 jit_solution(4238834285950384875)
XLA Ops:
  0.0 15.4 %fourier_analysis.1 = bf16[128,8,1360]{2,1,0:T(8,128)(2,1)} custom-call(s32[512]{0:T(512)} %ids_ref.1, bf16[1360,2560]{1,0:T(8,128)(2,1)} %bitcast.17), custom_call_target="tpu_custom_call" | custom-call | flops 7130316800 | bytes 10485760 | tf_op jit(solution)/shard_map/fourier_analysis/pallas_call | solution.py:76
  15.4 11.9 %all-to-all-start = ((bf16[128,8,1360]{2,1,0:T(8,128)(2,1)}), bf16[128,8,1360]{2,1,0:T(8,128)(2,1)}, u32[]{:S(2)}, u32[]{:S(2)}) async-start(bf16[128,8,1360]{2,1,0:T(8,128)(2,1)} %fourier_analysis.1), calls=%async_computation | async-start | bytes 5767168 | tf_op jit(solution)/shard_map/all_to_all | solution.py:426
  27.4 1.3 %dynamic_slice.3.ids_ref = s32[4]{0:T(128)} dynamic-slice(s32[512]{0:T(512)} %ids_ref.1, s32[]{:T(128)S(6)} %select_n.142), dynamic_slice_sizes={4} | dynamic-slice | bytes 36 | tf_op jit(solution)/shard_map/dynamic_slice | solution.py:404
  28.7 0.6 broadcast_in_dim.3.map_ref
  29.3 14.0 %degrees_first.1.refs_6_.refs_2_ = bf16[160,136,256]{2,1,0:T(8,128)(2,1)} custom-call(bf16[136,136,160]{2,1,0:T(8,128)(2,1)} %bitcast.16), custom_call_target="tpu_custom_call" | custom-call | flops 1000000000 | bytes 30000000 | tf_op jit(solution)/shard_map/degrees_first/pallas_call | solution.py:283
  43.3 19.2 %arrange_legendre.1.leg_hbm = bf16[4,1280,1280]{2,1,0:T(8,128)(2,1)} custom-call(s32[4]{0:T(128)} %dynamic_slice.3.ids_ref, s32[1,1280]{1,0:T(1,128)} %broadcast_in_dim.3.map_ref, bf16[4,1280,1280]{2,1,0:T(8,128)(2,1)} %leg_ref.1), custom_call_target="tpu_custom_call" | custom-call | flops 16777216000 | bytes 26214400 | tf_op jit(solution)/shard_map/arrange_legendre/pallas_call | solution.py:113
  62.5 0.6 stack.54.dests_ref
  63.1 2.6 %all-to-all-done = bf16[128,8,1360]{2,1,0:T(8,128)(2,1)} async-done(((bf16[128,8,1360]{2,1,0:T(8,128)(2,1)}), bf16[128,8,1360]{2,1,0:T(8,128)(2,1)}, u32[]{:S(2)}, u32[]{:S(2)}) %all-to-all-start) | async-done | bytes 2785312 | tf_op jit(solution)/shard_map/all_to_all | solution.py:426
  65.7 12.7 %legendre_sums.1 = (bf16[1360,128]{1,0:T(8,128)(2,1)}, bf16[1360,128]{1,0:T(8,128)(2,1)}, bf16[1360,128]{1,0:T(8,128)(2,1)}, bf16[1360,128]{1,0:T(8,128)(2,1)}, ...) custom-call(s32[4]{0:T(128)} %dynamic_slice.3.ids_ref, ...), custom_call_target="tpu_custom_call" | custom-call | flops 3000000000 | bytes 20971520 | tf_op jit(solution)/shard_map/legendre_sums/pallas_call | solution.py:229
  78.5 0.3 collective-permute-start
  78.8 1.1 collective-permute-start.1
  80.0 2.9 %collective-permute-start.2 = (bf16[1360,128]{1,0:T(8,128)(2,1)}, bf16[1360,128]{1,0:T(8,128)(2,1)S(1)}, u32[]{:S(2)}, u32[]{:S(2)}) collective-permute-start(bf16[1360,128]{1,0:T(8,128)(2,1)} %get-tuple-element.30), channel_id=1, source_target_pairs={{0,6},{1,7},{2,0},{3,1},{4,2},{5,3},{6,4},{7,5},{8,14},{9,15},{10,... | collective-permute-start | bytes 1044488 | tf_op jit(solution)/shard_map/ppermute | solution.py:435
  82.8 0.4 collective-permute-start.3
  83.2 1.1 collective-permute-start.6
  84.4 4.1 %collective-permute-done.refs_2_ = bf16[1360,128]{1,0:T(8,128)(2,1)S(1)} collective-permute-done((bf16[1360,128]{1,0:T(8,128)(2,1)}, bf16[1360,128]{1,0:T(8,128)(2,1)S(1)}, u32[]{:S(2)}, u32[]{:S(2)}) %collective-permute-start) | collective-permute-done | bytes 348192 | tf_op jit(solution)/shard_map/ppermute | solution.py:435
  88.5 8.8 %collective-permute-done.1.refs_3_ = bf16[1360,128]{1,0:T(8,128)(2,1)S(1)} collective-permute-done((bf16[1360,128]{1,0:T(8,128)(2,1)}, bf16[1360,128]{1,0:T(8,128)(2,1)S(1)}, u32[]{:S(2)}, u32[]{:S(2)}) %collective-permute-start.1) | collective-permute-done | bytes 348192 | tf_op jit(solution)/shard_map/ppermute | solution.py:435
  97.3 1.0 collective-permute-done.3.refs_5_
  98.3 2.4 %collective-permute-start.4 = (bf16[1360,128]{1,0:T(8,128)(2,1)}, bf16[1360,128]{1,0:T(8,128)(2,1)}, u32[]{:S(2)}, u32[]{:S(2)}) collective-permute-start(bf16[1360,128]{1,0:T(8,128)(2,1)} %get-tuple-element.34), channel_id=1, source_target_pairs={{0,4},{1,5},{2,6},{3,7},{4,0},{5,1},{6,2},{7,3},{8,12},{9,13},{10,... | collective-permute-start | bytes 1044488 | tf_op jit(solution)/shard_map/ppermute | solution.py:435
  100.7 1.4 %collective-permute-start.5 = (bf16[1360,128]{1,0:T(8,128)(2,1)}, bf16[1360,128]{1,0:T(8,128)(2,1)}, u32[]{:S(2)}, u32[]{:S(2)}) collective-permute-start(bf16[1360,128]{1,0:T(8,128)(2,1)} %get-tuple-element.35), channel_id=1, source_target_pairs={{0,5},{1,4},{2,7},{3,6},{4,1},{5,0},{6,3},{7,2},{8,13},{9,12},{10,... | collective-permute-start | bytes 1044488 | tf_op jit(solution)/shard_map/ppermute | solution.py:435
  102.1 0.6 stack.57.place_ref
  102.7 0.6 pad_add_fusion.place_ref
  103.3 0.7 copy-done.4
  104.1 13.8 %vertical_covariance.2.refs_3_ = f32[32,2,136,160]{3,2,1,0:T(8,128)} custom-call(s32[6]{0:T(128)} %stack.57.place_ref, bf16[1360,128]{1,0:T(8,128)(2,1)} %copy-done.4, bf16[1360,128]{1,0:T(8,128)(2,1)} %get-tuple-element.38.refs_1_, bf16[1360,128]{1,0:T(8,128)(2,1)} %copy-done, bf16[1360,128]{1,0:T(8,128)(2,1)} %copy-done.1, bf16[1360,128]{1,0:T(8,128)(2,1)} %copy-done.2, ...), custom_call_target="tpu_custom_call" | custom-call | flops 2000000000 | bytes 16777216 | tf_op jit(solution)/shard_map/vertical_covariance/pallas_call | solution.py:368
  117.9 10.3 %vertical_covariance.3 = f32[32,2,136,160]{3,2,1,0:T(8,128)} custom-call(s32[2]{0:T(128)} %pad_add_fusion.place_ref, bf16[1360,128]{1,0:T(8,128)(2,1)} %collective-permute-done.4.refs_0_, bf16[1360,128]{1,0:T(8,128)(2,1)} %collective-permute-done.5.refs_1_, bf16[160,136,256]{2,1,0:T(8,128)(2,1)} %degrees_first.1.refs_6_.refs_2_, ...), custom_call_target="tpu_custom_call", output_to_operand_aliasing={{}: (4, {})} | custom-call | flops 2000000000 | bytes 16777216 | tf_op jit(solution)/shard_map/vertical_covariance/pallas_call | solution.py:368
  (15 shorter events, 0.0 us)
Async XLA Ops:
  0.0 28.7 %copy-start.5 = (s32[1280]{0:T(1024)S(1)}, s32[1280]{0:T(1024)}, u32[]{:S(2)}) copy-start(s32[1280]{0:T(1024)} %param.9) | copy-start | bytes 15364
  15.4 50.4 %all-to-all-start = ((bf16[128,8,1360]{2,1,0:T(8,128)(2,1)}), bf16[128,8,1360]{2,1,0:T(8,128)(2,1)}, u32[]{:S(2)}, u32[]{:S(2)}) async-start(bf16[128,8,1360]{2,1,0:T(8,128)(2,1)} %fourier_analysis.1), calls=%async_computation | async-start | bytes 5767168 | tf_op jit(solution)/shard_map/all_to_all | solution.py:426
  78.5 10.0 %collective-permute-start = (bf16[1360,128]{1,0:T(8,128)(2,1)}, bf16[1360,128]{1,0:T(8,128)(2,1)S(1)}, u32[]{:S(2)}, u32[]{:S(2)}) collective-permute-start(bf16[1360,128]{1,0:T(8,128)(2,1)} %get-tuple-element.28), channel_id=1, source_target_pairs={{0,2},{1,3},{2,4},{3,5},{4,6},{5,7},{6,0},{7,1},{8,10},{9,11},{10,... | collective-permute-start | bytes 1044488 | tf_op jit(solution)/shard_map/ppermute | solution.py:435
  78.8 18.5 %collective-permute-start.1 = (bf16[1360,128]{1,0:T(8,128)(2,1)}, bf16[1360,128]{1,0:T(8,128)(2,1)S(1)}, u32[]{:S(2)}, u32[]{:S(2)}) collective-permute-start(bf16[1360,128]{1,0:T(8,128)(2,1)} %get-tuple-element.29), channel_id=1, source_target_pairs={{0,3},{1,2},{2,5},{3,4},{4,7},{5,6},{6,1},{7,0},{8,11},{9,10},{10,... | collective-permute-start | bytes 1044488 | tf_op jit(solution)/shard_map/ppermute | solution.py:435
  80.0 17.3 %collective-permute-start.2 = (bf16[1360,128]{1,0:T(8,128)(2,1)}, bf16[1360,128]{1,0:T(8,128)(2,1)S(1)}, u32[]{:S(2)}, u32[]{:S(2)}) collective-permute-start(bf16[1360,128]{1,0:T(8,128)(2,1)} %get-tuple-element.30), channel_id=1, source_target_pairs={{0,6},{1,7},{2,0},{3,1},{4,2},{5,3},{6,4},{7,5},{8,14},{9,15},{10,... | collective-permute-start | bytes 1044488 | tf_op jit(solution)/shard_map/ppermute | solution.py:435
  82.8 15.5 %collective-permute-start.3 = (bf16[1360,128]{1,0:T(8,128)(2,1)}, bf16[1360,128]{1,0:T(8,128)(2,1)S(1)}, u32[]{:S(2)}, u32[]{:S(2)}) collective-permute-start(bf16[1360,128]{1,0:T(8,128)(2,1)} %get-tuple-element.31), channel_id=1, source_target_pairs={{0,7},{1,6},{2,1},{3,0},{4,3},{5,2},{6,5},{7,4},{8,15},{9,14},{10,... | collective-permute-start | bytes 1044488 | tf_op jit(solution)/shard_map/ppermute | solution.py:435
  83.2 20.1 %collective-permute-start.6 = (bf16[1360,128]{1,0:T(8,128)(2,1)}, bf16[1360,128]{1,0:T(8,128)(2,1)S(1)}, u32[]{:S(2)}, u32[]{:S(2)}) collective-permute-start(bf16[1360,128]{1,0:T(8,128)(2,1)} %get-tuple-element.37), channel_id=1, source_target_pairs={{0,1},{1,0},{2,3},{3,2},{4,5},{5,4},{6,7},{7,6},{8,9},{9,8},{10,11... | collective-permute-start | bytes 1044488 | tf_op jit(solution)/shard_map/ppermute | solution.py:435
  88.5 14.9 %copy-start = (bf16[1360,128]{1,0:T(8,128)(2,1)}, bf16[1360,128]{1,0:T(8,128)(2,1)S(1)}, u32[]{:S(2)}) copy-start(bf16[1360,128]{1,0:T(8,128)(2,1)S(1)} %collective-permute-done.refs_2_) | copy-start | bytes 1044484
  97.3 6.0 %copy-start.1 = (bf16[1360,128]{1,0:T(8,128)(2,1)}, bf16[1360,128]{1,0:T(8,128)(2,1)S(1)}, u32[]{:S(2)}) copy-start(bf16[1360,128]{1,0:T(8,128)(2,1)S(1)} %collective-permute-done.1.refs_3_) | copy-start | bytes 1044484
  97.3 6.0 %copy-start.2 = (bf16[1360,128]{1,0:T(8,128)(2,1)}, bf16[1360,128]{1,0:T(8,128)(2,1)S(1)}, u32[]{:S(2)}) copy-start(bf16[1360,128]{1,0:T(8,128)(2,1)S(1)} %collective-permute-done.2.refs_4_) | copy-start | bytes 1044484
  98.3 5.0 %copy-start.3 = (bf16[1360,128]{1,0:T(8,128)(2,1)}, bf16[1360,128]{1,0:T(8,128)(2,1)S(1)}, u32[]{:S(2)}) copy-start(bf16[1360,128]{1,0:T(8,128)(2,1)S(1)} %collective-permute-done.3.refs_5_) | copy-start | bytes 1044484
  98.3 19.6 %collective-permute-start.4 = (bf16[1360,128]{1,0:T(8,128)(2,1)}, bf16[1360,128]{1,0:T(8,128)(2,1)}, u32[]{:S(2)}, u32[]{:S(2)}) collective-permute-start(bf16[1360,128]{1,0:T(8,128)(2,1)} %get-tuple-element.34), channel_id=1, source_target_pairs={{0,4},{1,5},{2,6},{3,7},{4,0},{5,1},{6,2},{7,3},{8,12},{9,13},{10,... | collective-permute-start | bytes 1044488 | tf_op jit(solution)/shard_map/ppermute | solution.py:435
  100.7 17.2 %collective-permute-start.5 = (bf16[1360,128]{1,0:T(8,128)(2,1)}, bf16[1360,128]{1,0:T(8,128)(2,1)}, u32[]{:S(2)}, u32[]{:S(2)}) collective-permute-start(bf16[1360,128]{1,0:T(8,128)(2,1)} %get-tuple-element.35), channel_id=1, source_target_pairs={{0,5},{1,4},{2,7},{3,6},{4,1},{5,0},{6,3},{7,2},{8,13},{9,12},{10,... | collective-permute-start | bytes 1044488 | tf_op jit(solution)/shard_map/ppermute | solution.py:435
  103.3 0.7 copy-start.4

commit v4 on v3

--- a/solution.py
+++ b/solution.py
@@ -252,7 +252,7 @@
     )(own_orders, dests, arrived, legendre)
 
 
-def degrees_first_kernel(cov_ref, out_ref, front, back):
+def degrees_first_kernel(cov_ref, out_ref, tail_ref, front, back):
     step = pl.program_id(0)
     group, levels, deg_block = cov_ref.shape
     last = pl.num_programs(0) - 1
@@ -269,23 +269,39 @@
     def _():
         def narrow(n, carry):
             rows = pl.ds(pl.multiple_of(n * levels, 8), levels)
-            out_ref[n, :, 0:128] = front[rows, :].astype(jnp.bfloat16)
-            out_ref[n, :, 128:] = back[rows, :].astype(jnp.bfloat16)
+            out_ref[n, 0:levels, :] = front[rows, :].astype(jnp.bfloat16)
             return carry
 
         lax.fori_loop(0, deg_block, narrow, 0, unroll=4)
+
+        def pack(g, carry):
+            total = back[pl.ds(pl.multiple_of(g * 16 * levels, 8), levels), :]
+            for i in range(1, 16):
+                rows = pl.ds(pl.multiple_of((g * 16 + i) * levels, 8), levels)
+                total = total + pltpu.roll(back[rows, :], 8 * i, 1)
+            tail_ref[g, 0:levels, :] = total.astype(jnp.bfloat16)
+            return carry
+
+        lax.fori_loop(0, deg_block // 16, pack, 0)
 
 
 def degrees_first(cov_levels):
     levels, _, deg_block = cov_levels.shape
     group = 17
     steps = levels // group
+    padded = -(-levels // 16) * 16
     return pl.pallas_call(
         degrees_first_kernel,
         grid=(steps + 1,),
         in_specs=[pl.BlockSpec((group, levels, deg_block), lambda s: (jnp.minimum(s, steps - 1), 0, 0))],
-        out_specs=pl.BlockSpec((deg_block, levels, 256), lambda s: (0, 0, 0), pipeline_mode=pl.Buffered(1)),
-        out_shape=jax.ShapeDtypeStruct((deg_block, levels, 256), jnp.bfloat16),
+        out_specs=[
+            pl.BlockSpec((deg_block, padded, 128), lambda s: (0, 0, 0), pipeline_mode=pl.Buffered(1)),
+            pl.BlockSpec((deg_block // 16, padded, 128), lambda s: (0, 0, 0), pipeline_mode=pl.Buffered(1)),
+        ],
+        out_shape=[
+            jax.ShapeDtypeStruct((deg_block, padded, 128), jnp.bfloat16),
+            jax.ShapeDtypeStruct((deg_block // 16, padded, 128), jnp.bfloat16),
+        ],
         scratch_shapes=[pltpu.VMEM((deg_block * levels, 128), jnp.float32)] * 2,
         compiler_params=pltpu.CompilerParams(vmem_limit_bytes=FULL),
         cost_estimate=pl.CostEstimate(flops=10**9, bytes_accessed=3 * 10**7, transcendentals=0),
@@ -294,10 +310,10 @@
 
 
 def covariance_kernel(place_ref, *refs, per, count, carried):
-    got_hbm, cov_hbm = refs[:count], refs[count]
-    out_ref, gots, cov, main, rest, out_main, out_rest, got_sems, cov_sems = refs[count + 1 + carried:]
+    got_hbm, cov_hbm, tail_hbm = refs[:count], refs[count], refs[count + 1]
+    out_ref, gots, cov, cov_tail, main, rest, out_main, out_rest, got_sems, cov_sems, tail_sem = refs[count + 2 + carried:]
     step = pl.program_id(0)
-    deg_block, levels, _ = cov.shape
+    deg_block, levels = out_ref.shape[3], out_ref.shape[2]
     pairs = 2 * per
     groups = 128 // (8 * pairs)
     chunk = deg_block // groups
@@ -317,7 +333,9 @@
     def _():
         for s in range(count):
             load_got(s).start()
-        for p in range(2):
+        load_tail = pltpu.make_async_copy(tail_hbm, cov_tail, tail_sem)
+        load_tail.start()
+        for p in range(4):
             load_cov(p).start()
         for s in range(count):
             load_got(s).wait()
@@ -331,24 +349,25 @@
                     moved = tail if lane == 0 else pltpu.roll(tail, 128 - lane, 1)
                     rest[base + g * chunk:base + (g + 1) * chunk, :] = moved
 
-        def multiply(n, carry):
-            left = jnp.concatenate([
-                main[pl.ds(n, rows, stride=pitch), :],
-                rest[pl.ds(n, rows, stride=pitch), :]], axis=1)[:, :levels].astype(jnp.bfloat16)
-            product = jnp.dot(left, cov[n], preferred_element_type=jnp.float32)
-            out_main[pl.ds(n, rows, stride=pitch), :] = product[:, :128]
-            out_rest[pl.ds(n, rows, stride=pitch), :] = product[:, 128:]
-            return carry
+        load_tail.wait()
 
         def share(p, carry):
             load_cov(p).wait()
 
-            @pl.when(p + 2 < pieces)
+            @pl.when(p + 4 < pieces)
             def _():
-                load_cov(p + 2).start()
+                load_cov(p + 4).start()
 
             for i in range(piece):
-                multiply(p * piece + i, carry)
+                n = p * piece + i
+                left = jnp.concatenate([
+                    main[pl.ds(n, rows, stride=pitch), :],
+                    rest[pl.ds(n, rows, stride=pitch), :]], axis=1)[:, :levels].astype(jnp.bfloat16)
+                right = jnp.concatenate([cov[n, 0:levels, :], cov_tail[p, 0:levels, :]], axis=1)
+                product = jnp.dot(left, right, preferred_element_type=jnp.float32)
+                out_main[pl.ds(n, rows, stride=pitch), :] = product[:, :128]
+                last = product[:, 128:]
+                out_rest[pl.ds(n, rows, stride=pitch), :] = last if i == 0 else pltpu.roll(last, 128 - 8 * i, 1)
             return carry
 
         lax.fori_loop(0, pieces, share, 0)
@@ -359,9 +378,9 @@
         out_ref[r // 2, r % 2, 128:, :] = out_rest[pl.ds(base, deg_block), :][:, :levels - 128].T
 
 
-def covariance(places, arrived, cov, out, orders, per, half, halves):
+def covariance(places, arrived, cov, cov_tail, out, orders, levels, per, half, halves):
     count = len(arrived)
-    deg_block, levels, wide = cov.shape
+    deg_block = cov.shape[0]
     rows = count * 2 * per * (deg_block + 8)
     carried = 0 if out is None else 1
     anywhere = pl.BlockSpec(memory_space=pl.ANY)
@@ -370,22 +389,24 @@
         grid_spec=pltpu.PrefetchScalarGridSpec(
             num_scalar_prefetch=1,
             grid=(count,),
-            in_specs=[anywhere] * (count + 1 + carried),
+            in_specs=[anywhere] * (count + 2 + carried),
             out_specs=pl.BlockSpec((per, 2, levels, deg_block), lambda s, place: (place[s] * halves + half, 0, 0, 0)),
             scratch_shapes=[
                 pltpu.VMEM((count,) + arrived[0].shape, jnp.bfloat16),
                 pltpu.VMEM(cov.shape, jnp.bfloat16),
+                pltpu.VMEM(cov_tail.shape, jnp.bfloat16),
             ] + [pltpu.VMEM((rows, 128), jnp.float32)] * 4 + [
                 pltpu.SemaphoreType.DMA((count,)),
-                pltpu.SemaphoreType.DMA((10,)),
+                pltpu.SemaphoreType.DMA((deg_block // 16,)),
+                pltpu.SemaphoreType.DMA,
             ],
         ),
         out_shape=jax.ShapeDtypeStruct((orders, 2, levels, deg_block), jnp.float32),
-        input_output_aliases={count + 2: 0} if carried else {},
+        input_output_aliases={count + 3: 0} if carried else {},
         compiler_params=pltpu.CompilerParams(vmem_limit_bytes=FULL),
         cost_estimate=pl.CostEstimate(flops=2 * 10**9, bytes_accessed=16 * MIB, transcendentals=0),
         name="vertical_covariance",
-    )(places, *arrived, cov, *([out] if carried else []))
+    )(places, *arrived, cov, cov_tail, *([out] if carried else []))
 
 
 HALVES = 1
@@ -417,36 +438,31 @@
     spectra = [fourier(grid_rows, order_ids, dests, per, 0)]
     spectra[0], cycle_map, cov_root = lax.optimization_barrier((spectra[0], cycle_map, cov_root))
     arranged = arrange_legendre(own_orders, cycle_map, legendre, 2 * degree_count // lev_count)
-    cov = degrees_first(cov_root.transpose(1, 2, 0))
-    arranged, cov = lax.optimization_barrier((arranged, cov))
-    arrived = []
-    for h in range(HALVES):
-        if h > 0:
-            spectra.append(fourier(grid_rows, order_ids, dests, per, h))
-        blocks = lax.all_to_all(spectra[h], ("ord", "lev"), split_axis=0, concat_axis=0, tiled=True)
-        blocks = blocks.reshape((ord_count, lev_count) + blocks.shape[1:])
-        packed = legendre_sums(own_orders, targets, blocks, arranged, per, h, lev_dev, cycles_dev)
-        sent = dict(zip(moves, packed))
-        got = {(0, 0): sent[0, 0]}
-
-        def exchange(some):
-            for d, f in some:
-                pairs = [(rank, moved(rank, d, f)) for rank in range(lev_count)]
-                got[d, f] = lax.ppermute(sent[d, f], "lev", pairs)
-
-        exchange(near + home[:1])
-        held = near + far
-        tied = lax.optimization_barrier([got[m] for m in near] + [sent[m] for m in far])
-        for m, block in zip(held, tied):
-            (got if m in near else sent)[m] = block
-        exchange(far)
-        arrived.append(got)
-
-    out = None
-    for h in range(HALVES):
-        for some in (home + near, far):
-            places = jnp.stack([moved(lev, chips - d, f) for d, f in some]).astype(jnp.int32)
-            out = covariance(places, [arrived[h][m] for m in some], cov, out, orders_dev * lev_count, per, h, HALVES)
+    cov, cov_tail = degrees_first(cov_root.transpose(1, 2, 0))
+    arranged, cov, cov_tail = lax.optimization_barrier((arranged, cov, cov_tail))
+    blocks = lax.all_to_all(spectra[0], ("ord", "lev"), split_axis=0, concat_axis=0, tiled=True)
+    blocks = blocks.reshape((ord_count, lev_count) + blocks.shape[1:])
+    packed = legendre_sums(own_orders, targets, blocks, arranged, per, 0, lev_dev, cycles_dev)
+    sent = dict(zip(moves, packed))
+    got = {(0, 0): sent[0, 0]}
+
+    def exchange(some):
+        for d, f in some:
+            pairs = [(rank, moved(rank, d, f)) for rank in range(lev_count)]
+            got[d, f] = lax.ppermute(sent[d, f], "lev", pairs)
+
+    def apply(some, out):
+        places = jnp.stack([moved(lev, chips - d, f) for d, f in some]).astype(jnp.int32)
+        return covariance(places, [got[m] for m in some], cov, cov_tail, out, orders_dev * lev_count, lev_dev * lev_count, per, 0, HALVES)
+
+    exchange(near + home[:1])
+    out = apply(home, None)
+    tied, out = lax.optimization_barrier(([got[m] for m in near] + [sent[m] for m in far], out))
+    for m, block in zip(near + far, tied):
+        (got if m in near else sent)[m] = block
+    exchange(far)
+    out = apply(near, out)
+    out = apply(far, out)
     return out.transpose(3, 0, 1, 2)
 
 

time: 129 us -> 127 us (0.984)
  waiting for transfers between devices: 16.5 us -> 11.2 us
  Pallas kernels: 85.4 us -> 87.7 us
    ppermute x7, waiting for transfers between devices: 13.9 us -> 8.85 us  [exchange(): got[d, f] = lax.ppermute(sent[d, f], 'lev', pairs)]
    pallas_call x2 -> x3, Pallas kernels: 24.1 us -> 26.1 us  [covariance(): pl.pallas_call(functools.partial(covariance_kernel, per=per, count=count,...]
  transfers between devices with their start and end apart: 8 -> 8, of which waited for: 4 -> 3; matrix products, arithmetic and copies ran while one was open for 3% -> 3% of each run, Pallas kernels for 37% -> 41%
where the time goes in v4:
time: 127 us; the launch traced here: 126 us
  Pallas kernels  87.7 us (69%)
  starting transfers between devices  21.6 us (17%)
  waiting for transfers between devices  11.2 us (9%)
  local copies, waits for them, and re-layouts  3.25 us (3%)
  other arithmetic  1.82 us (1%)
    pallas_call x3, Pallas kernels, covariance(): pl.pallas_call(functools.partial(covariance_kernel, per=per, count=count,...  26.1 us
    pallas_call x1, Pallas kernels, arrange_legendre(): pl.pallas_call(arrange_kernel, grid_spec=pltpu.PrefetchScalarGridSpec(num...  18.5 us
    pallas_call x1, Pallas kernels, fourier(): pl.pallas_call(kernel, grid_spec=pltpu.PrefetchScalarGridSpec(num_scalar_...  15.4 us
    pallas_call x1, Pallas kernels, degrees_first(): pl.pallas_call(degrees_first_kernel, grid=(steps + 1,), in_specs=[pl.Bloc...  15 us
    pallas_call x1, Pallas kernels, legendre_sums(): pl.pallas_call(kernel, grid_spec=pltpu.PrefetchScalarGridSpec(num_scalar_...  12.7 us
    all_to_all x1, starting transfers between devices, shards(): lax.all_to_all(spectra[0], ('ord', 'lev'), split_axis=0, concat_axis=0, t...  11.9 us
    ppermute x7, starting transfers between devices, exchange(): got[d, f] = lax.ppermute(sent[d, f], 'lev', pairs)  9.66 us
    ppermute x7, waiting for transfers between devices, exchange(): got[d, f] = lax.ppermute(sent[d, f], 'lev', pairs)  8.85 us
  transfers between devices with their start and end apart: 8, of which 3 were waited for; matrix products, arithmetic and copies ran while one was open for 3% of the time, Pallas kernels for 41%

profile of v4, /device:TPU:1, one launch (start us, length us, event | category | flops | bytes accessed | tf_op | source)
XLA Modules:
  0.0 125.9 jit_solution(12808287654456659537)
XLA Ops:
  0.0 15.4 %fourier_analysis.1 = bf16[128,8,1360]{2,1,0:T(8,128)(2,1)} custom-call(s32[512]{0:T(512)} %ids_ref.1, bf16[1360,2560]{1,0:T(8,128)(2,1)} %bitcast.17), custom_call_target="tpu_custom_call" | custom-call | flops 7130316800 | bytes 10485760 | tf_op jit(solution)/shard_map/fourier_analysis/pallas_call | solution.py:76
  15.4 11.9 %all-to-all-start = ((bf16[128,8,1360]{2,1,0:T(8,128)(2,1)}), bf16[128,8,1360]{2,1,0:T(8,128)(2,1)}, u32[]{:S(2)}, u32[]{:S(2)}) async-start(bf16[128,8,1360]{2,1,0:T(8,128)(2,1)} %fourier_analysis.1), calls=%async_computation | async-start | bytes 5767168 | tf_op jit(solution)/shard_map/all_to_all | solution.py:443
  27.4 1.3 %dynamic_slice.3.ids_ref = s32[4]{0:T(128)} dynamic-slice(s32[512]{0:T(512)} %ids_ref.1, s32[]{:T(128)S(6)} %select_n.142), dynamic_slice_sizes={4} | dynamic-slice | bytes 36 | tf_op jit(solution)/shard_map/dynamic_slice | solution.py:425
  28.7 0.6 broadcast_in_dim.3.map_ref
  29.3 15.0 %degrees_first.1 = (bf16[160,144,128]{2,1,0:T(8,128)(2,1)}, bf16[10,144,128]{2,1,0:T(8,128)(2,1)}) custom-call(bf16[136,136,160]{2,1,0:T(8,128)(2,1)} %bitcast.16), custom_call_target="tpu_custom_call" | custom-call | flops 1000000000 | bytes 30000000 | tf_op jit(solution)/shard_map/degrees_first/pallas_call | solution.py:293
  44.3 18.5 %arrange_legendre.1.leg_hbm = bf16[4,1280,1280]{2,1,0:T(8,128)(2,1)} custom-call(s32[4]{0:T(128)} %dynamic_slice.3.ids_ref, s32[1,1280]{1,0:T(1,128)} %broadcast_in_dim.3.map_ref, bf16[4,1280,1280]{2,1,0:T(8,128)(2,1)} %leg_ref.1), custom_call_target="tpu_custom_call" | custom-call | flops 16777216000 | bytes 26214400 | tf_op jit(solution)/shard_map/arrange_legendre/pallas_call | solution.py:113
  62.8 0.6 stack.57.dests_ref
  63.4 2.3 %all-to-all-done = bf16[128,8,1360]{2,1,0:T(8,128)(2,1)} async-done(((bf16[128,8,1360]{2,1,0:T(8,128)(2,1)}), bf16[128,8,1360]{2,1,0:T(8,128)(2,1)}, u32[]{:S(2)}, u32[]{:S(2)}) %all-to-all-start) | async-done | bytes 2785312 | tf_op jit(solution)/shard_map/all_to_all | solution.py:443
  65.7 12.7 %legendre_sums.1 = (bf16[1360,128]{1,0:T(8,128)(2,1)}, bf16[1360,128]{1,0:T(8,128)(2,1)}, bf16[1360,128]{1,0:T(8,128)(2,1)}, bf16[1360,128]{1,0:T(8,128)(2,1)}, ...) custom-call(s32[4]{0:T(128)} %dynamic_slice.3.ids_ref, ...), custom_call_target="tpu_custom_call" | custom-call | flops 3000000000 | bytes 20971520 | tf_op jit(solution)/shard_map/legendre_sums/pallas_call | solution.py:229
  78.5 1.2 collective-permute-start.4
  79.7 0.3 collective-permute-start
  80.2 2.7 %collective-permute-start.2 = (bf16[1360,128]{1,0:T(8,128)(2,1)}, bf16[1360,128]{1,0:T(8,128)(2,1)S(1)}, u32[]{:S(2)}, u32[]{:S(2)}) collective-permute-start(bf16[1360,128]{1,0:T(8,128)(2,1)} %get-tuple-element.36), channel_id=1, source_target_pairs={{0,6},{1,7},{2,0},{3,1},{4,2},{5,3},{6,4},{7,5},{8,14},{9,15},{10,... | collective-permute-start | bytes 1044488 | tf_op jit(solution)/shard_map/ppermute | solution.py:452
  82.9 1.5 %collective-permute-start.3 = (bf16[1360,128]{1,0:T(8,128)(2,1)}, bf16[1360,128]{1,0:T(8,128)(2,1)S(1)}, u32[]{:S(2)}, u32[]{:S(2)}) collective-permute-start(bf16[1360,128]{1,0:T(8,128)(2,1)} %get-tuple-element.37), channel_id=1, source_target_pairs={{0,7},{1,6},{2,1},{3,0},{4,3},{5,2},{6,5},{7,4},{8,15},{9,14},{10,... | collective-permute-start | bytes 1044488 | tf_op jit(solution)/shard_map/ppermute | solution.py:452
  84.4 0.6 pad_add_fusion.1.place_ref
  85.0 0.7 copy-done.4
  85.8 8.0 %vertical_covariance.3.refs_6_ = f32[32,2,136,160]{3,2,1,0:T(8,128)} custom-call(s32[2]{0:T(128)} %pad_add_fusion.1.place_ref, bf16[1360,128]{1,0:T(8,128)(2,1)} %copy-done.4, bf16[1360,128]{1,0:T(8,128)(2,1)} %get-tuple-element.41.refs_1_, bf16[160,144,128]{2,1,0:T(8,128)(2,1)} %get-tuple-element.42.refs_2_.refs_4_, ...), custom_call_target="tpu_custom_call" | custom-call | flops 2000000000 | bytes 16777216 | tf_op jit(solution)/shard_map/vertical_covariance/pallas_call | solution.py:387
  93.8 4.7 %collective-permute-done.1.refs_1_ = bf16[1360,128]{1,0:T(8,128)(2,1)S(1)} collective-permute-done((bf16[1360,128]{1,0:T(8,128)(2,1)}, bf16[1360,128]{1,0:T(8,128)(2,1)S(1)}, u32[]{:S(2)}, u32[]{:S(2)}) %collective-permute-start.1) | collective-permute-done | bytes 348192 | tf_op jit(solution)/shard_map/ppermute | solution.py:452
  98.5 2.9 %collective-permute-start.5 = (bf16[1360,128]{1,0:T(8,128)(2,1)}, bf16[1360,128]{1,0:T(8,128)(2,1)S(1)}, u32[]{:S(2)}, u32[]{:S(2)}) collective-permute-start(bf16[1360,128]{1,0:T(8,128)(2,1)} %get-tuple-element.44), channel_id=1, source_target_pairs={{0,4},{1,5},{2,6},{3,7},{4,0},{5,1},{6,2},{7,3},{8,12},{9,13},{10,... | collective-permute-start | bytes 1044488 | tf_op jit(solution)/shard_map/ppermute | solution.py:452
  101.4 0.8 collective-permute-start.6
  102.2 0.7 pad_add_fusion.2.place_ref
  102.8 0.6 pad_add_fusion.place_ref
  103.4 10.1 %vertical_covariance.4.refs_4_ = f32[32,2,136,160]{3,2,1,0:T(8,128)} custom-call(s32[4]{0:T(128)} %pad_add_fusion.2.place_ref, bf16[1360,128]{1,0:T(8,128)(2,1)} %copy-done, bf16[1360,128]{1,0:T(8,128)(2,1)} %copy-done.1, bf16[1360,128]{1,0:T(8,128)(2,1)} %copy-done.2, bf16[1360,128]{1,0:T(8,128)(2,1)} %copy-done.3, ...), custom_call_target="tpu_custom_call", output_to_operand_aliasing={{}: (7, {})} | custom-call | flops 2000000000 | bytes 16777216 | tf_op jit(solution)/shard_map/vertical_covariance/pallas_call | solution.py:387
  113.5 4.2 %collective-permute-done.6.refs_1_ = bf16[1360,128]{1,0:T(8,128)(2,1)} collective-permute-done((bf16[1360,128]{1,0:T(8,128)(2,1)}, bf16[1360,128]{1,0:T(8,128)(2,1)}, u32[]{:S(2)}, u32[]{:S(2)}) %collective-permute-start.6) | collective-permute-done | bytes 348192 | tf_op jit(solution)/shard_map/ppermute | solution.py:452
  117.7 8.0 %vertical_covariance.5 = f32[32,2,136,160]{3,2,1,0:T(8,128)} custom-call(s32[2]{0:T(128)} %pad_add_fusion.place_ref, bf16[1360,128]{1,0:T(8,128)(2,1)} %copy-done.5, bf16[1360,128]{1,0:T(8,128)(2,1)} %collective-permute-done.6.refs_1_, bf16[160,144,128]{2,1,0:T(8,128)(2,1)} %get-tuple-element.42.refs_2_.refs_4_, ...), custom_call_target="tpu_custom_call", output_to_operand_aliasing={{}: (5, {})} | custom-call | flops 2000000000 | bytes 16777216 | tf_op jit(solution)/shard_map/vertical_covariance/pallas_call | solution.py:387
  (19 shorter events, 0.3 us)
Async XLA Ops:
  0.0 28.7 %copy-start.6 = (s32[1280]{0:T(1024)S(1)}, s32[1280]{0:T(1024)}, u32[]{:S(2)}) copy-start(s32[1280]{0:T(1024)} %param.9) | copy-start | bytes 15364
  15.4 50.4 %all-to-all-start = ((bf16[128,8,1360]{2,1,0:T(8,128)(2,1)}), bf16[128,8,1360]{2,1,0:T(8,128)(2,1)}, u32[]{:S(2)}, u32[]{:S(2)}) async-start(bf16[128,8,1360]{2,1,0:T(8,128)(2,1)} %fourier_analysis.1), calls=%async_computation | async-start | bytes 5767168 | tf_op jit(solution)/shard_map/all_to_all | solution.py:443
  78.5 6.5 %collective-permute-start.4 = (bf16[1360,128]{1,0:T(8,128)(2,1)}, bf16[1360,128]{1,0:T(8,128)(2,1)S(1)}, u32[]{:S(2)}, u32[]{:S(2)}) collective-permute-start(bf16[1360,128]{1,0:T(8,128)(2,1)} %get-tuple-element.40), channel_id=1, source_target_pairs={{0,1},{1,0},{2,3},{3,2},{4,5},{5,4},{6,7},{7,6},{8,9},{9,8},{10,11... | collective-permute-start | bytes 1044488 | tf_op jit(solution)/shard_map/ppermute | solution.py:452
  79.7 14.1 %collective-permute-start = (bf16[1360,128]{1,0:T(8,128)(2,1)}, bf16[1360,128]{1,0:T(8,128)(2,1)S(1)}, u32[]{:S(2)}, u32[]{:S(2)}) collective-permute-start(bf16[1360,128]{1,0:T(8,128)(2,1)} %get-tuple-element.34), channel_id=1, source_target_pairs={{0,2},{1,3},{2,4},{3,5},{4,6},{5,7},{6,0},{7,1},{8,10},{9,11},{10,... | collective-permute-start | bytes 1044488 | tf_op jit(solution)/shard_map/ppermute | solution.py:452
  80.0 18.5 %collective-permute-start.1 = (bf16[1360,128]{1,0:T(8,128)(2,1)}, bf16[1360,128]{1,0:T(8,128)(2,1)S(1)}, u32[]{:S(2)}, u32[]{:S(2)}) collective-permute-start(bf16[1360,128]{1,0:T(8,128)(2,1)} %get-tuple-element.35), channel_id=1, source_target_pairs={{0,3},{1,2},{2,5},{3,4},{4,7},{5,6},{6,1},{7,0},{8,11},{9,10},{10,... | collective-permute-start | bytes 1044488 | tf_op jit(solution)/shard_map/ppermute | solution.py:452
  80.2 18.2 %collective-permute-start.2 = (bf16[1360,128]{1,0:T(8,128)(2,1)}, bf16[1360,128]{1,0:T(8,128)(2,1)S(1)}, u32[]{:S(2)}, u32[]{:S(2)}) collective-permute-start(bf16[1360,128]{1,0:T(8,128)(2,1)} %get-tuple-element.36), channel_id=1, source_target_pairs={{0,6},{1,7},{2,0},{3,1},{4,2},{5,3},{6,4},{7,5},{8,14},{9,15},{10,... | collective-permute-start | bytes 1044488 | tf_op jit(solution)/shard_map/ppermute | solution.py:452
  82.9 15.6 %collective-permute-start.3 = (bf16[1360,128]{1,0:T(8,128)(2,1)}, bf16[1360,128]{1,0:T(8,128)(2,1)S(1)}, u32[]{:S(2)}, u32[]{:S(2)}) collective-permute-start(bf16[1360,128]{1,0:T(8,128)(2,1)} %get-tuple-element.37), channel_id=1, source_target_pairs={{0,7},{1,6},{2,1},{3,0},{4,3},{5,2},{6,5},{7,4},{8,15},{9,14},{10,... | collective-permute-start | bytes 1044488 | tf_op jit(solution)/shard_map/ppermute | solution.py:452
  85.0 0.7 copy-start.4
  93.8 9.6 %copy-start = (bf16[1360,128]{1,0:T(8,128)(2,1)}, bf16[1360,128]{1,0:T(8,128)(2,1)S(1)}, u32[]{:S(2)}) copy-start(bf16[1360,128]{1,0:T(8,128)(2,1)S(1)} %collective-permute-done.refs_0_) | copy-start | bytes 1044484
  98.5 5.0 %copy-start.1 = (bf16[1360,128]{1,0:T(8,128)(2,1)}, bf16[1360,128]{1,0:T(8,128)(2,1)S(1)}, u32[]{:S(2)}) copy-start(bf16[1360,128]{1,0:T(8,128)(2,1)S(1)} %collective-permute-done.1.refs_1_) | copy-start | bytes 1044484
  98.5 5.0 %copy-start.2 = (bf16[1360,128]{1,0:T(8,128)(2,1)}, bf16[1360,128]{1,0:T(8,128)(2,1)S(1)}, u32[]{:S(2)}) copy-start(bf16[1360,128]{1,0:T(8,128)(2,1)S(1)} %collective-permute-done.2.refs_2_) | copy-start | bytes 1044484
  98.5 5.0 %copy-start.3 = (bf16[1360,128]{1,0:T(8,128)(2,1)}, bf16[1360,128]{1,0:T(8,128)(2,1)S(1)}, u32[]{:S(2)}) copy-start(bf16[1360,128]{1,0:T(8,128)(2,1)S(1)} %collective-permute-done.3.refs_3_) | copy-start | bytes 1044484
  98.5 15.0 %collective-permute-start.5 = (bf16[1360,128]{1,0:T(8,128)(2,1)}, bf16[1360,128]{1,0:T(8,128)(2,1)S(1)}, u32[]{:S(2)}, u32[]{:S(2)}) collective-permute-start(bf16[1360,128]{1,0:T(8,128)(2,1)} %get-tuple-element.44), channel_id=1, source_target_pairs={{0,4},{1,5},{2,6},{3,7},{4,0},{5,1},{6,2},{7,3},{8,12},{9,13},{10,... | collective-permute-start | bytes 1044488 | tf_op jit(solution)/shard_map/ppermute | solution.py:452
  101.4 16.3 %collective-permute-start.6 = (bf16[1360,128]{1,0:T(8,128)(2,1)}, bf16[1360,128]{1,0:T(8,128)(2,1)}, u32[]{:S(2)}, u32[]{:S(2)}) collective-permute-start(bf16[1360,128]{1,0:T(8,128)(2,1)} %get-tuple-element.45), channel_id=1, source_target_pairs={{0,5},{1,4},{2,7},{3,6},{4,1},{5,0},{6,3},{7,2},{8,13},{9,12},{10,... | collective-permute-start | bytes 1044488 | tf_op jit(solution)/shard_map/ppermute | solution.py:452
  113.5 4.2 %copy-start.5 = (bf16[1360,128]{1,0:T(8,128)(2,1)}, bf16[1360,128]{1,0:T(8,128)(2,1)S(1)}, u32[]{:S(2)}) copy-start(bf16[1360,128]{1,0:T(8,128)(2,1)S(1)} %collective-permute-done.5.refs_0_) | copy-start | bytes 1044484

commit v5 on v4

--- a/solution.py
+++ b/solution.py
@@ -378,7 +378,7 @@
         out_ref[r // 2, r % 2, 128:, :] = out_rest[pl.ds(base, deg_block), :][:, :levels - 128].T
 
 
-def covariance(places, arrived, cov, cov_tail, out, orders, levels, per, half, halves):
+def covariance(places, first, arrived, cov, cov_tail, out, orders, levels, per, half, halves):
     count = len(arrived)
     deg_block = cov.shape[0]
     rows = count * 2 * per * (deg_block + 8)
@@ -390,7 +390,7 @@
             num_scalar_prefetch=1,
             grid=(count,),
             in_specs=[anywhere] * (count + 2 + carried),
-            out_specs=pl.BlockSpec((per, 2, levels, deg_block), lambda s, place: (place[s] * halves + half, 0, 0, 0)),
+            out_specs=pl.BlockSpec((per, 2, levels, deg_block), lambda s, place: (place[first + s] * halves + half, 0, 0, 0)),
             scratch_shapes=[
                 pltpu.VMEM((count,) + arrived[0].shape, jnp.bfloat16),
                 pltpu.VMEM(cov.shape, jnp.bfloat16),
@@ -451,14 +451,18 @@
             pairs = [(rank, moved(rank, d, f)) for rank in range(lev_count)]
             got[d, f] = lax.ppermute(sent[d, f], "lev", pairs)
 
+    turns = home + near + far
+    places = jnp.stack([moved(lev, chips - d, f) for d, f in turns]).astype(jnp.int32)
+
     def apply(some, out):
-        places = jnp.stack([moved(lev, chips - d, f) for d, f in some]).astype(jnp.int32)
-        return covariance(places, [got[m] for m in some], cov, cov_tail, out, orders_dev * lev_count, lev_dev * lev_count, per, 0, HALVES)
+        first = turns.index(some[0])
+        return covariance(places, first, [got[m] for m in some], cov, cov_tail, out, orders_dev * lev_count, lev_dev * lev_count, per, 0, HALVES)
 
     exchange(near + home[:1])
     out = apply(home, None)
-    tied, out = lax.optimization_barrier(([got[m] for m in near] + [sent[m] for m in far], out))
-    for m, block in zip(near + far, tied):
+    ahead = near[:len(near) // 2]
+    tied, out = lax.optimization_barrier(([got[m] for m in ahead] + [sent[m] for m in far], out))
+    for m, block in zip(ahead + far, tied):
         (got if m in near else sent)[m] = block
     exchange(far)
     out = apply(near, out)

time: 127 us -> 127 us (level)
  local copies, waits for them, and re-layouts: 3.25 us -> 5.28 us
  other arithmetic: 1.82 us -> 0 us
    another operation x3 -> x0, other arithmetic: 1.82 us -> none  [apply(): jnp.stack([moved(lev, chips - d, f) for d, f in some]).astype(jnp.int32)]
    unnamed x14, local copies, waits for them, and re-layouts: 0.77 us -> 2.19 us
  transfers between devices with their start and end apart: 8 -> 8, of which waited for: 3 -> 3; matrix products, arithmetic and copies ran while one was open for 3% -> 2% of each run, Pallas kernels for 41% -> 42%
where the time goes in v5:
time: 127 us; the launch traced here: 126 us
  Pallas kernels  88.4 us (70%)
  starting transfers between devices  21.2 us (17%)
  waiting for transfers between devices  10.6 us (8%)
  local copies, waits for them, and re-layouts  5.28 us (4%)
    pallas_call x3, Pallas kernels, covariance(): pl.pallas_call(functools.partial(covariance_kernel, per=per, count=count,...  26.1 us
    pallas_call x1, Pallas kernels, arrange_legendre(): pl.pallas_call(arrange_kernel, grid_spec=pltpu.PrefetchScalarGridSpec(num...  19.2 us
    pallas_call x1, Pallas kernels, fourier(): pl.pallas_call(kernel, grid_spec=pltpu.PrefetchScalarGridSpec(num_scalar_...  15.4 us
    pallas_call x1, Pallas kernels, degrees_first(): pl.pallas_call(degrees_first_kernel, grid=(steps + 1,), in_specs=[pl.Bloc...  15 us
    pallas_call x1, Pallas kernels, legendre_sums(): pl.pallas_call(kernel, grid_spec=pltpu.PrefetchScalarGridSpec(num_scalar_...  12.7 us
    all_to_all x1, starting transfers between devices, shards(): lax.all_to_all(spectra[0], ('ord', 'lev'), split_axis=0, concat_axis=0, t...  11.9 us
    ppermute x7, starting transfers between devices, exchange(): got[d, f] = lax.ppermute(sent[d, f], 'lev', pairs)  9.31 us
    ppermute x7, waiting for transfers between devices, exchange(): got[d, f] = lax.ppermute(sent[d, f], 'lev', pairs)  8.9 us
  transfers between devices with their start and end apart: 8, of which 3 were waited for; matrix products, arithmetic and copies ran while one was open for 2% of the time, Pallas kernels for 42%

profile of v5, /device:TPU:1, one launch (start us, length us, event | category | flops | bytes accessed | tf_op | source)
XLA Modules:
  0.0 125.8 jit_solution(606257785754389099)
XLA Ops:
  0.0 15.4 %fourier_analysis.1 = bf16[128,8,1360]{2,1,0:T(8,128)(2,1)} custom-call(s32[512]{0:T(512)} %ids_ref.1, bf16[1360,2560]{1,0:T(8,128)(2,1)} %bitcast.17), custom_call_target="tpu_custom_call" | custom-call | flops 7130316800 | bytes 10485760 | tf_op jit(solution)/shard_map/fourier_analysis/pallas_call | solution.py:76
  15.4 11.9 %all-to-all-start = ((bf16[128,8,1360]{2,1,0:T(8,128)(2,1)}), bf16[128,8,1360]{2,1,0:T(8,128)(2,1)}, u32[]{:S(2)}, u32[]{:S(2)}) async-start(bf16[128,8,1360]{2,1,0:T(8,128)(2,1)} %fourier_analysis.1), calls=%async_computation | async-start | bytes 5767168 | tf_op jit(solution)/shard_map/all_to_all | solution.py:443
  27.4 1.3 %dynamic_slice.3.ids_ref = s32[4]{0:T(128)} dynamic-slice(s32[512]{0:T(512)} %ids_ref.1, s32[]{:T(128)S(6)} %select_n.145), dynamic_slice_sizes={4} | dynamic-slice | bytes 36 | tf_op jit(solution)/shard_map/dynamic_slice | solution.py:425
  28.7 0.6 broadcast_in_dim.3.map_ref
  29.3 15.0 %degrees_first.1 = (bf16[160,144,128]{2,1,0:T(8,128)(2,1)}, bf16[10,144,128]{2,1,0:T(8,128)(2,1)}) custom-call(bf16[136,136,160]{2,1,0:T(8,128)(2,1)} %bitcast.16), custom_call_target="tpu_custom_call" | custom-call | flops 1000000000 | bytes 30000000 | tf_op jit(solution)/shard_map/degrees_first/pallas_call | solution.py:293
  44.3 19.2 %arrange_legendre.1.leg_hbm = bf16[4,1280,1280]{2,1,0:T(8,128)(2,1)} custom-call(s32[4]{0:T(128)} %dynamic_slice.3.ids_ref, s32[1,1280]{1,0:T(1,128)} %broadcast_in_dim.3.map_ref, bf16[4,1280,1280]{2,1,0:T(8,128)(2,1)} %leg_ref.1), custom_call_target="tpu_custom_call" | custom-call | flops 16777216000 | bytes 26214400 | tf_op jit(solution)/shard_map/arrange_legendre/pallas_call | solution.py:113
  63.5 0.6 stack.53.dests_ref
  64.1 1.7 %all-to-all-done = bf16[128,8,1360]{2,1,0:T(8,128)(2,1)} async-done(((bf16[128,8,1360]{2,1,0:T(8,128)(2,1)}), bf16[128,8,1360]{2,1,0:T(8,128)(2,1)}, u32[]{:S(2)}, u32[]{:S(2)}) %all-to-all-start) | async-done | bytes 2785312 | tf_op jit(solution)/shard_map/all_to_all | solution.py:443
  65.7 12.7 %legendre_sums.1 = (bf16[1360,128]{1,0:T(8,128)(2,1)}, bf16[1360,128]{1,0:T(8,128)(2,1)}, bf16[1360,128]{1,0:T(8,128)(2,1)}, bf16[1360,128]{1,0:T(8,128)(2,1)}, ...) custom-call(s32[4]{0:T(128)} %dynamic_slice.3.ids_ref, ...), custom_call_target="tpu_custom_call" | custom-call | flops 3000000000 | bytes 20971520 | tf_op jit(solution)/shard_map/legendre_sums/pallas_call | solution.py:229
  78.5 1.2 collective-permute-start.2
  79.7 0.3 collective-permute-start
  80.0 0.1 collective-permute-start.1
  80.2 0.6 stack.50.place_ref
  80.8 2.8 %collective-permute-start.5 = (bf16[1360,128]{1,0:T(8,128)(2,1)}, bf16[1360,128]{1,0:T(8,128)(2,1)S(1)}, u32[]{:S(2)}, u32[]{:S(2)}) collective-permute-start(bf16[1360,128]{1,0:T(8,128)(2,1)} %get-tuple-element.44), channel_id=1, source_target_pairs={{0,6},{1,7},{2,0},{3,1},{4,2},{5,3},{6,4},{7,5},{8,14},{9,15},{10,... | collective-permute-start | bytes 1044488 | tf_op jit(solution)/shard_map/ppermute | solution.py:452
  83.5 1.5 %collective-permute-start.6 = (bf16[1360,128]{1,0:T(8,128)(2,1)}, bf16[1360,128]{1,0:T(8,128)(2,1)S(1)}, u32[]{:S(2)}, u32[]{:S(2)}) collective-permute-start(bf16[1360,128]{1,0:T(8,128)(2,1)} %get-tuple-element.45), channel_id=1, source_target_pairs={{0,7},{1,6},{2,1},{3,0},{4,3},{5,2},{6,5},{7,4},{8,15},{9,14},{10,... | collective-permute-start | bytes 1044488 | tf_op jit(solution)/shard_map/ppermute | solution.py:452
  85.0 0.7 copy-done.2
  85.8 8.0 %vertical_covariance.3.refs_6_ = f32[32,2,136,160]{3,2,1,0:T(8,128)} custom-call(s32[8]{0:T(128)} %stack.50.place_ref, bf16[1360,128]{1,0:T(8,128)(2,1)} %copy-done.2, bf16[1360,128]{1,0:T(8,128)(2,1)} %get-tuple-element.37.refs_1_, bf16[160,144,128]{2,1,0:T(8,128)(2,1)} %get-tuple-element.38.refs_2_.refs_4_, ...), custom_call_target="tpu_custom_call" | custom-call | flops 2000000000 | bytes 16777216 | tf_op jit(solution)/shard_map/vertical_covariance/pallas_call | solution.py:387
  93.8 4.6 %collective-permute-done.1.refs_1_ = bf16[1360,128]{1,0:T(8,128)(2,1)S(1)} collective-permute-done((bf16[1360,128]{1,0:T(8,128)(2,1)}, bf16[1360,128]{1,0:T(8,128)(2,1)S(1)}, u32[]{:S(2)}, u32[]{:S(2)}) %collective-permute-start.1) | collective-permute-done | bytes 348192 | tf_op jit(solution)/shard_map/ppermute | solution.py:452
  98.5 3.4 %collective-permute-start.4 = (bf16[1360,128]{1,0:T(8,128)(2,1)}, bf16[1360,128]{1,0:T(8,128)(2,1)}, u32[]{:S(2)}, u32[]{:S(2)}) collective-permute-start(bf16[1360,128]{1,0:T(8,128)(2,1)} %get-tuple-element.41), channel_id=1, source_target_pairs={{0,5},{1,4},{2,7},{3,6},{4,1},{5,0},{6,3},{7,2},{8,13},{9,12},{10,... | collective-permute-start | bytes 1044488 | tf_op jit(solution)/shard_map/ppermute | solution.py:452
  101.9 0.7 copy-done.3
  102.6 0.7 copy-done.4
  103.3 10.1 %vertical_covariance.4.refs_4_ = f32[32,2,136,160]{3,2,1,0:T(8,128)} custom-call(s32[8]{0:T(128)} %stack.50.place_ref, bf16[1360,128]{1,0:T(8,128)(2,1)} %copy-done, bf16[1360,128]{1,0:T(8,128)(2,1)} %copy-done.1, bf16[1360,128]{1,0:T(8,128)(2,1)} %copy-done.3, bf16[1360,128]{1,0:T(8,128)(2,1)} %copy-done.4, ...), custom_call_target="tpu_custom_call", output_to_operand_aliasing={{}: (7, {})} | custom-call | flops 2000000000 | bytes 16777216 | tf_op jit(solution)/shard_map/vertical_covariance/pallas_call | solution.py:387
  113.4 4.3 %collective-permute-done.4.refs_1_ = bf16[1360,128]{1,0:T(8,128)(2,1)} collective-permute-done((bf16[1360,128]{1,0:T(8,128)(2,1)}, bf16[1360,128]{1,0:T(8,128)(2,1)}, u32[]{:S(2)}, u32[]{:S(2)}) %collective-permute-start.4) | collective-permute-done | bytes 348192 | tf_op jit(solution)/shard_map/ppermute | solution.py:452
  117.6 8.0 %vertical_covariance.5 = f32[32,2,136,160]{3,2,1,0:T(8,128)} custom-call(s32[8]{0:T(128)} %stack.50.place_ref, bf16[1360,128]{1,0:T(8,128)(2,1)} %copy-done.5, bf16[1360,128]{1,0:T(8,128)(2,1)} %collective-permute-done.4.refs_1_, bf16[160,144,128]{2,1,0:T(8,128)(2,1)} %get-tuple-element.38.refs_2_.refs_4_, ...), custom_call_target="tpu_custom_call", output_to_operand_aliasing={{}: (5, {})} | custom-call | flops 2000000000 | bytes 16777216 | tf_op jit(solution)/shard_map/vertical_covariance/pallas_call | solution.py:387
  (17 shorter events, 0.0 us)
Async XLA Ops:
  0.0 28.7 %copy-start.6 = (s32[1280]{0:T(1024)S(1)}, s32[1280]{0:T(1024)}, u32[]{:S(2)}) copy-start(s32[1280]{0:T(1024)} %param.9) | copy-start | bytes 15364
  15.4 50.4 %all-to-all-start = ((bf16[128,8,1360]{2,1,0:T(8,128)(2,1)}), bf16[128,8,1360]{2,1,0:T(8,128)(2,1)}, u32[]{:S(2)}, u32[]{:S(2)}) async-start(bf16[128,8,1360]{2,1,0:T(8,128)(2,1)} %fourier_analysis.1), calls=%async_computation | async-start | bytes 5767168 | tf_op jit(solution)/shard_map/all_to_all | solution.py:443
  78.5 6.6 %collective-permute-start.2 = (bf16[1360,128]{1,0:T(8,128)(2,1)}, bf16[1360,128]{1,0:T(8,128)(2,1)S(1)}, u32[]{:S(2)}, u32[]{:S(2)}) collective-permute-start(bf16[1360,128]{1,0:T(8,128)(2,1)} %get-tuple-element.36), channel_id=1, source_target_pairs={{0,1},{1,0},{2,3},{3,2},{4,5},{5,4},{6,7},{7,6},{8,9},{9,8},{10,11... | collective-permute-start | bytes 1044488 | tf_op jit(solution)/shard_map/ppermute | solution.py:452
  79.7 14.1 %collective-permute-start = (bf16[1360,128]{1,0:T(8,128)(2,1)}, bf16[1360,128]{1,0:T(8,128)(2,1)S(1)}, u32[]{:S(2)}, u32[]{:S(2)}) collective-permute-start(bf16[1360,128]{1,0:T(8,128)(2,1)} %get-tuple-element.32), channel_id=1, source_target_pairs={{0,2},{1,3},{2,4},{3,5},{4,6},{5,7},{6,0},{7,1},{8,10},{9,11},{10,... | collective-permute-start | bytes 1044488 | tf_op jit(solution)/shard_map/ppermute | solution.py:452
  80.0 18.5 %collective-permute-start.1 = (bf16[1360,128]{1,0:T(8,128)(2,1)}, bf16[1360,128]{1,0:T(8,128)(2,1)S(1)}, u32[]{:S(2)}, u32[]{:S(2)}) collective-permute-start(bf16[1360,128]{1,0:T(8,128)(2,1)} %get-tuple-element.33), channel_id=1, source_target_pairs={{0,3},{1,2},{2,5},{3,4},{4,7},{5,6},{6,1},{7,0},{8,11},{9,10},{10,... | collective-permute-start | bytes 1044488 | tf_op jit(solution)/shard_map/ppermute | solution.py:452
  80.8 21.1 %collective-permute-start.5 = (bf16[1360,128]{1,0:T(8,128)(2,1)}, bf16[1360,128]{1,0:T(8,128)(2,1)S(1)}, u32[]{:S(2)}, u32[]{:S(2)}) collective-permute-start(bf16[1360,128]{1,0:T(8,128)(2,1)} %get-tuple-element.44), channel_id=1, source_target_pairs={{0,6},{1,7},{2,0},{3,1},{4,2},{5,3},{6,4},{7,5},{8,14},{9,15},{10,... | collective-permute-start | bytes 1044488 | tf_op jit(solution)/shard_map/ppermute | solution.py:452
  83.5 18.3 %collective-permute-start.6 = (bf16[1360,128]{1,0:T(8,128)(2,1)}, bf16[1360,128]{1,0:T(8,128)(2,1)S(1)}, u32[]{:S(2)}, u32[]{:S(2)}) collective-permute-start(bf16[1360,128]{1,0:T(8,128)(2,1)} %get-tuple-element.45), channel_id=1, source_target_pairs={{0,7},{1,6},{2,1},{3,0},{4,3},{5,2},{6,5},{7,4},{8,15},{9,14},{10,... | collective-permute-start | bytes 1044488 | tf_op jit(solution)/shard_map/ppermute | solution.py:452
  85.0 0.7 copy-start.2
  93.8 8.0 %copy-start = (bf16[1360,128]{1,0:T(8,128)(2,1)}, bf16[1360,128]{1,0:T(8,128)(2,1)S(1)}, u32[]{:S(2)}) copy-start(bf16[1360,128]{1,0:T(8,128)(2,1)S(1)} %collective-permute-done.refs_0_) | copy-start | bytes 1044484
  98.5 3.4 %copy-start.1 = (bf16[1360,128]{1,0:T(8,128)(2,1)}, bf16[1360,128]{1,0:T(8,128)(2,1)S(1)}, u32[]{:S(2)}) copy-start(bf16[1360,128]{1,0:T(8,128)(2,1)S(1)} %collective-permute-done.1.refs_1_) | copy-start | bytes 1044484
  98.5 14.9 %collective-permute-start.3 = (bf16[1360,128]{1,0:T(8,128)(2,1)}, bf16[1360,128]{1,0:T(8,128)(2,1)S(1)}, u32[]{:S(2)}, u32[]{:S(2)}) collective-permute-start(bf16[1360,128]{1,0:T(8,128)(2,1)} %get-tuple-element.40), channel_id=1, source_target_pairs={{0,4},{1,5},{2,6},{3,7},{4,0},{5,1},{6,2},{7,3},{8,12},{9,13},{10,... | collective-permute-start | bytes 1044488 | tf_op jit(solution)/shard_map/ppermute | solution.py:452
  98.5 19.2 %collective-permute-start.4 = (bf16[1360,128]{1,0:T(8,128)(2,1)}, bf16[1360,128]{1,0:T(8,128)(2,1)}, u32[]{:S(2)}, u32[]{:S(2)}) collective-permute-start(bf16[1360,128]{1,0:T(8,128)(2,1)} %get-tuple-element.41), channel_id=1, source_target_pairs={{0,5},{1,4},{2,7},{3,6},{4,1},{5,0},{6,3},{7,2},{8,13},{9,12},{10,... | collective-permute-start | bytes 1044488 | tf_op jit(solution)/shard_map/ppermute | solution.py:452
  101.8 0.7 copy-start.3
  102.6 0.7 copy-start.4
  113.4 4.3 %copy-start.5 = (bf16[1360,128]{1,0:T(8,128)(2,1)}, bf16[1360,128]{1,0:T(8,128)(2,1)S(1)}, u32[]{:S(2)}) copy-start(bf16[1360,128]{1,0:T(8,128)(2,1)S(1)} %collective-permute-done.3.refs_0_) | copy-start | bytes 1044484

commit v6 on v5

--- a/solution.py
+++ b/solution.py
@@ -71,7 +71,7 @@
     points, lon_count = grid_rows.shape
     orders_dev = order_ids.shape[0] // dests
     rows = 2 * dests * per
-    steps = per
+    steps = per // 2
     kernel = functools.partial(fourier_kernel, orders_dev=orders_dev, per=per, half=half)
     return pl.pallas_call(
         kernel,
@@ -460,9 +460,8 @@
 
     exchange(near + home[:1])
     out = apply(home, None)
-    ahead = near[:len(near) // 2]
-    tied, out = lax.optimization_barrier(([got[m] for m in ahead] + [sent[m] for m in far], out))
-    for m, block in zip(ahead + far, tied):
+    tied, out = lax.optimization_barrier(([got[m] for m in near] + [sent[m] for m in far], out))
+    for m, block in zip(near + far, tied):
         (got if m in near else sent)[m] = block
     exchange(far)
     out = apply(near, out)

time: 127 us -> 126 us (level)
  local copies, waits for them, and re-layouts: 5.28 us -> 3.86 us
    unnamed x14, local copies, waits for them, and re-layouts: 2.19 us -> 0.77 us
where the time goes in v6:
time: 126 us
  Pallas kernels  88.3 us (70%)
  starting transfers between devices  21.6 us (17%)
  waiting for transfers between devices  11.6 us (9%)
  local copies, waits for them, and re-layouts  3.86 us (3%)
    pallas_call x3, Pallas kernels, covariance(): pl.pallas_call(functools.partial(covariance_kernel, per=per, count=count,...  26.1 us
    pallas_call x1, Pallas kernels, arrange_legendre(): pl.pallas_call(arrange_kernel, grid_spec=pltpu.PrefetchScalarGridSpec(num...  19.3 us
    pallas_call x1, Pallas kernels, fourier(): pl.pallas_call(kernel, grid_spec=pltpu.PrefetchScalarGridSpec(num_scalar_...  15.2 us
    pallas_call x1, Pallas kernels, degrees_first(): pl.pallas_call(degrees_first_kernel, grid=(steps + 1,), in_specs=[pl.Bloc...  15 us
    pallas_call x1, Pallas kernels, legendre_sums(): pl.pallas_call(kernel, grid_spec=pltpu.PrefetchScalarGridSpec(num_scalar_...  12.7 us
    all_to_all x1, starting transfers between devices, shards(): lax.all_to_all(spectra[0], ('ord', 'lev'), split_axis=0, concat_axis=0, t...  11.9 us
    ppermute x7, waiting for transfers between devices, exchange(): got[d, f] = lax.ppermute(sent[d, f], 'lev', pairs)  10.1 us
    ppermute x7, starting transfers between devices, exchange(): got[d, f] = lax.ppermute(sent[d, f], 'lev', pairs)  9.66 us
  transfers between devices with their start and end apart: 8, of which 3 were waited for; matrix products, arithmetic and copies ran while one was open for 2% of the time, Pallas kernels for 42%

profile of v6, /device:TPU:1, one launch (start us, length us, event | category | flops | bytes accessed | tf_op | source)
XLA Modules:
  0.0 125.7 jit_solution(635834726460351432)
XLA Ops:
  0.0 15.2 %fourier_analysis.1 = bf16[128,8,1360]{2,1,0:T(8,128)(2,1)} custom-call(s32[512]{0:T(512)} %ids_ref.1, bf16[1360,2560]{1,0:T(8,128)(2,1)} %bitcast.17), custom_call_target="tpu_custom_call" | custom-call | flops 7130316800 | bytes 10485760 | tf_op jit(solution)/shard_map/fourier_analysis/pallas_call | solution.py:76
  15.2 11.9 %all-to-all-start = ((bf16[128,8,1360]{2,1,0:T(8,128)(2,1)}), bf16[128,8,1360]{2,1,0:T(8,128)(2,1)}, u32[]{:S(2)}, u32[]{:S(2)}) async-start(bf16[128,8,1360]{2,1,0:T(8,128)(2,1)} %fourier_analysis.1), calls=%async_computation | async-start | bytes 5767168 | tf_op jit(solution)/shard_map/all_to_all | solution.py:443
  27.2 1.3 %dynamic_slice.3.ids_ref = s32[4]{0:T(128)} dynamic-slice(s32[512]{0:T(512)} %ids_ref.1, s32[]{:T(128)S(6)} %select_n.145), dynamic_slice_sizes={4} | dynamic-slice | bytes 36 | tf_op jit(solution)/shard_map/dynamic_slice | solution.py:425
  28.5 0.6 broadcast_in_dim.3.map_ref
  29.1 15.0 %degrees_first.1 = (bf16[160,144,128]{2,1,0:T(8,128)(2,1)}, bf16[10,144,128]{2,1,0:T(8,128)(2,1)}) custom-call(bf16[136,136,160]{2,1,0:T(8,128)(2,1)} %bitcast.16), custom_call_target="tpu_custom_call" | custom-call | flops 1000000000 | bytes 30000000 | tf_op jit(solution)/shard_map/degrees_first/pallas_call | solution.py:293
  44.1 19.3 %arrange_legendre.1.leg_hbm = bf16[4,1280,1280]{2,1,0:T(8,128)(2,1)} custom-call(s32[4]{0:T(128)} %dynamic_slice.3.ids_ref, s32[1,1280]{1,0:T(1,128)} %broadcast_in_dim.3.map_ref, bf16[4,1280,1280]{2,1,0:T(8,128)(2,1)} %leg_ref.1), custom_call_target="tpu_custom_call" | custom-call | flops 16777216000 | bytes 26214400 | tf_op jit(solution)/shard_map/arrange_legendre/pallas_call | solution.py:113
  63.4 0.6 stack.53.dests_ref
  64.0 1.6 %all-to-all-done = bf16[128,8,1360]{2,1,0:T(8,128)(2,1)} async-done(((bf16[128,8,1360]{2,1,0:T(8,128)(2,1)}), bf16[128,8,1360]{2,1,0:T(8,128)(2,1)}, u32[]{:S(2)}, u32[]{:S(2)}) %all-to-all-start) | async-done | bytes 2785312 | tf_op jit(solution)/shard_map/all_to_all | solution.py:443
  65.6 12.7 %legendre_sums.1 = (bf16[1360,128]{1,0:T(8,128)(2,1)}, bf16[1360,128]{1,0:T(8,128)(2,1)}, bf16[1360,128]{1,0:T(8,128)(2,1)}, bf16[1360,128]{1,0:T(8,128)(2,1)}, ...) custom-call(s32[4]{0:T(128)} %dynamic_slice.3.ids_ref, ...), custom_call_target="tpu_custom_call" | custom-call | flops 3000000000 | bytes 20971520 | tf_op jit(solution)/shard_map/legendre_sums/pallas_call | solution.py:229
  78.3 1.2 collective-permute-start.4
  79.5 0.3 collective-permute-start
  79.8 0.1 collective-permute-start.1
  80.0 2.8 %collective-permute-start.2 = (bf16[1360,128]{1,0:T(8,128)(2,1)}, bf16[1360,128]{1,0:T(8,128)(2,1)S(1)}, u32[]{:S(2)}, u32[]{:S(2)}) collective-permute-start(bf16[1360,128]{1,0:T(8,128)(2,1)} %get-tuple-element.36), channel_id=1, source_target_pairs={{0,6},{1,7},{2,0},{3,1},{4,2},{5,3},{6,4},{7,5},{8,14},{9,15},{10,... | collective-permute-start | bytes 1044488 | tf_op jit(solution)/shard_map/ppermute | solution.py:452
  82.7 1.5 %collective-permute-start.3 = (bf16[1360,128]{1,0:T(8,128)(2,1)}, bf16[1360,128]{1,0:T(8,128)(2,1)S(1)}, u32[]{:S(2)}, u32[]{:S(2)}) collective-permute-start(bf16[1360,128]{1,0:T(8,128)(2,1)} %get-tuple-element.37), channel_id=1, source_target_pairs={{0,7},{1,6},{2,1},{3,0},{4,3},{5,2},{6,5},{7,4},{8,15},{9,14},{10,... | collective-permute-start | bytes 1044488 | tf_op jit(solution)/shard_map/ppermute | solution.py:452
  84.2 0.6 stack.50.place_ref
  84.8 0.0 collective-permute-done.4.refs_0_
  84.8 0.7 copy-done.4
  85.6 8.0 %vertical_covariance.3.refs_6_ = f32[32,2,136,160]{3,2,1,0:T(8,128)} custom-call(s32[8]{0:T(128)} %stack.50.place_ref, bf16[1360,128]{1,0:T(8,128)(2,1)} %copy-done.4, bf16[1360,128]{1,0:T(8,128)(2,1)} %get-tuple-element.41.refs_1_, bf16[160,144,128]{2,1,0:T(8,128)(2,1)} %get-tuple-element.42.refs_2_.refs_4_, ...), custom_call_target="tpu_custom_call" | custom-call | flops 2000000000 | bytes 16777216 | tf_op jit(solution)/shard_map/vertical_covariance/pallas_call | solution.py:387
  93.6 4.6 %collective-permute-done.1.refs_1_ = bf16[1360,128]{1,0:T(8,128)(2,1)S(1)} collective-permute-done((bf16[1360,128]{1,0:T(8,128)(2,1)}, bf16[1360,128]{1,0:T(8,128)(2,1)S(1)}, u32[]{:S(2)}, u32[]{:S(2)}) %collective-permute-start.1) | collective-permute-done | bytes 348192 | tf_op jit(solution)/shard_map/ppermute | solution.py:452
  98.3 2.9 %collective-permute-start.5 = (bf16[1360,128]{1,0:T(8,128)(2,1)}, bf16[1360,128]{1,0:T(8,128)(2,1)S(1)}, u32[]{:S(2)}, u32[]{:S(2)}) collective-permute-start(bf16[1360,128]{1,0:T(8,128)(2,1)} %get-tuple-element.44), channel_id=1, source_target_pairs={{0,4},{1,5},{2,6},{3,7},{4,0},{5,1},{6,2},{7,3},{8,12},{9,13},{10,... | collective-permute-start | bytes 1044488 | tf_op jit(solution)/shard_map/ppermute | solution.py:452
  101.2 0.8 collective-permute-start.6
  102.0 10.1 %vertical_covariance.4.refs_4_ = f32[32,2,136,160]{3,2,1,0:T(8,128)} custom-call(s32[8]{0:T(128)} %stack.50.place_ref, bf16[1360,128]{1,0:T(8,128)(2,1)} %copy-done, bf16[1360,128]{1,0:T(8,128)(2,1)} %copy-done.1, bf16[1360,128]{1,0:T(8,128)(2,1)} %copy-done.2, bf16[1360,128]{1,0:T(8,128)(2,1)} %copy-done.3, ...), custom_call_target="tpu_custom_call", output_to_operand_aliasing={{}: (7, {})} | custom-call | flops 2000000000 | bytes 16777216 | tf_op jit(solution)/shard_map/vertical_covariance/pallas_call | solution.py:387
  112.1 5.4 %collective-permute-done.6.refs_1_ = bf16[1360,128]{1,0:T(8,128)(2,1)} collective-permute-done((bf16[1360,128]{1,0:T(8,128)(2,1)}, bf16[1360,128]{1,0:T(8,128)(2,1)}, u32[]{:S(2)}, u32[]{:S(2)}) %collective-permute-start.6) | collective-permute-done | bytes 348192 | tf_op jit(solution)/shard_map/ppermute | solution.py:452
  117.5 8.0 %vertical_covariance.5 = f32[32,2,136,160]{3,2,1,0:T(8,128)} custom-call(s32[8]{0:T(128)} %stack.50.place_ref, bf16[1360,128]{1,0:T(8,128)(2,1)} %copy-done.5, bf16[1360,128]{1,0:T(8,128)(2,1)} %collective-permute-done.6.refs_1_, bf16[160,144,128]{2,1,0:T(8,128)(2,1)} %get-tuple-element.42.refs_2_.refs_4_, ...), custom_call_target="tpu_custom_call", output_to_operand_aliasing={{}: (5, {})} | custom-call | flops 2000000000 | bytes 16777216 | tf_op jit(solution)/shard_map/vertical_covariance/pallas_call | solution.py:387
  (17 shorter events, 0.0 us)
Async XLA Ops:
  0.0 28.5 %copy-start.6 = (s32[1280]{0:T(1024)S(1)}, s32[1280]{0:T(1024)}, u32[]{:S(2)}) copy-start(s32[1280]{0:T(1024)} %param.9) | copy-start | bytes 15364
  15.2 50.3 %all-to-all-start = ((bf16[128,8,1360]{2,1,0:T(8,128)(2,1)}), bf16[128,8,1360]{2,1,0:T(8,128)(2,1)}, u32[]{:S(2)}, u32[]{:S(2)}) async-start(bf16[128,8,1360]{2,1,0:T(8,128)(2,1)} %fourier_analysis.1), calls=%async_computation | async-start | bytes 5767168 | tf_op jit(solution)/shard_map/all_to_all | solution.py:443
  78.3 6.6 %collective-permute-start.4 = (bf16[1360,128]{1,0:T(8,128)(2,1)}, bf16[1360,128]{1,0:T(8,128)(2,1)S(1)}, u32[]{:S(2)}, u32[]{:S(2)}) collective-permute-start(bf16[1360,128]{1,0:T(8,128)(2,1)} %get-tuple-element.40), channel_id=1, source_target_pairs={{0,1},{1,0},{2,3},{3,2},{4,5},{5,4},{6,7},{7,6},{8,9},{9,8},{10,11... | collective-permute-start | bytes 1044488 | tf_op jit(solution)/shard_map/ppermute | solution.py:452
  79.5 14.1 %collective-permute-start = (bf16[1360,128]{1,0:T(8,128)(2,1)}, bf16[1360,128]{1,0:T(8,128)(2,1)S(1)}, u32[]{:S(2)}, u32[]{:S(2)}) collective-permute-start(bf16[1360,128]{1,0:T(8,128)(2,1)} %get-tuple-element.34), channel_id=1, source_target_pairs={{0,2},{1,3},{2,4},{3,5},{4,6},{5,7},{6,0},{7,1},{8,10},{9,11},{10,... | collective-permute-start | bytes 1044488 | tf_op jit(solution)/shard_map/ppermute | solution.py:452
  79.8 18.5 %collective-permute-start.1 = (bf16[1360,128]{1,0:T(8,128)(2,1)}, bf16[1360,128]{1,0:T(8,128)(2,1)S(1)}, u32[]{:S(2)}, u32[]{:S(2)}) collective-permute-start(bf16[1360,128]{1,0:T(8,128)(2,1)} %get-tuple-element.35), channel_id=1, source_target_pairs={{0,3},{1,2},{2,5},{3,4},{4,7},{5,6},{6,1},{7,0},{8,11},{9,10},{10,... | collective-permute-start | bytes 1044488 | tf_op jit(solution)/shard_map/ppermute | solution.py:452
  80.0 18.3 %collective-permute-start.2 = (bf16[1360,128]{1,0:T(8,128)(2,1)}, bf16[1360,128]{1,0:T(8,128)(2,1)S(1)}, u32[]{:S(2)}, u32[]{:S(2)}) collective-permute-start(bf16[1360,128]{1,0:T(8,128)(2,1)} %get-tuple-element.36), channel_id=1, source_target_pairs={{0,6},{1,7},{2,0},{3,1},{4,2},{5,3},{6,4},{7,5},{8,14},{9,15},{10,... | collective-permute-start | bytes 1044488 | tf_op jit(solution)/shard_map/ppermute | solution.py:452
  82.7 15.6 %collective-permute-start.3 = (bf16[1360,128]{1,0:T(8,128)(2,1)}, bf16[1360,128]{1,0:T(8,128)(2,1)S(1)}, u32[]{:S(2)}, u32[]{:S(2)}) collective-permute-start(bf16[1360,128]{1,0:T(8,128)(2,1)} %get-tuple-element.37), channel_id=1, source_target_pairs={{0,7},{1,6},{2,1},{3,0},{4,3},{5,2},{6,5},{7,4},{8,15},{9,14},{10,... | collective-permute-start | bytes 1044488 | tf_op jit(solution)/shard_map/ppermute | solution.py:452
  84.8 0.7 copy-start.4
  93.6 8.4 %copy-start = (bf16[1360,128]{1,0:T(8,128)(2,1)}, bf16[1360,128]{1,0:T(8,128)(2,1)S(1)}, u32[]{:S(2)}) copy-start(bf16[1360,128]{1,0:T(8,128)(2,1)S(1)} %collective-permute-done.refs_0_) | copy-start | bytes 1044484
  98.3 3.7 %copy-start.1 = (bf16[1360,128]{1,0:T(8,128)(2,1)}, bf16[1360,128]{1,0:T(8,128)(2,1)S(1)}, u32[]{:S(2)}) copy-start(bf16[1360,128]{1,0:T(8,128)(2,1)S(1)} %collective-permute-done.1.refs_1_) | copy-start | bytes 1044484
  98.3 3.7 %copy-start.2 = (bf16[1360,128]{1,0:T(8,128)(2,1)}, bf16[1360,128]{1,0:T(8,128)(2,1)S(1)}, u32[]{:S(2)}) copy-start(bf16[1360,128]{1,0:T(8,128)(2,1)S(1)} %collective-permute-done.2.refs_2_) | copy-start | bytes 1044484
  98.3 3.7 %copy-start.3 = (bf16[1360,128]{1,0:T(8,128)(2,1)}, bf16[1360,128]{1,0:T(8,128)(2,1)S(1)}, u32[]{:S(2)}) copy-start(bf16[1360,128]{1,0:T(8,128)(2,1)S(1)} %collective-permute-done.3.refs_3_) | copy-start | bytes 1044484
  98.3 13.8 %collective-permute-start.5 = (bf16[1360,128]{1,0:T(8,128)(2,1)}, bf16[1360,128]{1,0:T(8,128)(2,1)S(1)}, u32[]{:S(2)}, u32[]{:S(2)}) collective-permute-start(bf16[1360,128]{1,0:T(8,128)(2,1)} %get-tuple-element.44), channel_id=1, source_target_pairs={{0,4},{1,5},{2,6},{3,7},{4,0},{5,1},{6,2},{7,3},{8,12},{9,13},{10,... | collective-permute-start | bytes 1044488 | tf_op jit(solution)/shard_map/ppermute | solution.py:452
  101.2 16.3 %collective-permute-start.6 = (bf16[1360,128]{1,0:T(8,128)(2,1)}, bf16[1360,128]{1,0:T(8,128)(2,1)}, u32[]{:S(2)}, u32[]{:S(2)}) collective-permute-start(bf16[1360,128]{1,0:T(8,128)(2,1)} %get-tuple-element.45), channel_id=1, source_target_pairs={{0,5},{1,4},{2,7},{3,6},{4,1},{5,0},{6,3},{7,2},{8,13},{9,12},{10,... | collective-permute-start | bytes 1044488 | tf_op jit(solution)/shard_map/ppermute | solution.py:452
  112.1 5.4 %copy-start.5 = (bf16[1360,128]{1,0:T(8,128)(2,1)}, bf16[1360,128]{1,0:T(8,128)(2,1)S(1)}, u32[]{:S(2)}) copy-start(bf16[1360,128]{1,0:T(8,128)(2,1)S(1)} %collective-permute-done.5.refs_0_) | copy-start | bytes 1044484
